TPU v7x, 32 devices: a whole 2x2x4 slice. The times are simulated.
32 devices in a mesh: groups: 2 (over x), gx: 4 (over y, core), gy: 4 (over z).
Axes of the slice: x: 2, y: 2, z: 4, core: 2. Of those that a mesh axis runs over, the one named last changes fastest.
Arguments:
- probes: bfloat16 [128, 16, 3, 512], P(('groups', 'gx', 'gy')), parts along dimension 0, may hold values from -6 to 6
- positions: float32 [128, 3, 512], P(('groups', 'gx', 'gy')), parts along dimension 0, may hold values from -4 to 130, as said below
- polar: float32 [128, 512], P(('groups', 'gx', 'gy')), parts along dimension 0, may hold values from 0.5 to 8
- basis: bfloat16 [128, 64, 3, 512], P(('groups', 'gx', 'gy')), parts along dimension 0, may hold values from -0.25 to 0.25
- leaf_transfer: bfloat16 [128, 64, 64], P(('groups', 'gx', 'gy')), parts along dimension 0, may hold values from -0.375 to 0.375
- cluster_transfer: bfloat16 [32, 64, 64], P(('groups', 'gx', 'gy')), parts along dimension 0, may hold values from -0.5 to 0.5
- upper_transfer: bfloat16 [24, 64, 64], P('groups'), parts along dimension 0, may hold values from -0.5 to 0.5
- cluster_coupling: bfloat16 [32, 6, 64, 64], P(('groups', 'gx', 'gy')), parts along dimension 0, may hold values from -0.3125 to 0.3125
- upper_coupling: bfloat16 [28, 6, 64, 64], P('groups'), parts along dimension 0, may hold values from -0.3125 to 0.3125
- near_lists: int32 [128, 6], P(('groups', 'gx', 'gy')), parts along dimension 0, may hold values from -1 to 63, as said below
- cluster_lists: int32 [32, 6], P(('groups', 'gx', 'gy')), parts along dimension 0, may hold values from 0 to 15, as said below
- upper_lists: int32 [28, 6], P('groups'), parts along dimension 0, may hold values from 0 to 7, as said below
Outputs:
- applied: bfloat16 [128, 16, 3, 512], P(('groups', 'gx', 'gy')), parts along dimension 0
There are 2 independent parts, one for each index of `groups`. A program takes and returns all parts, laid end to end along the dimension named above; each array names one. Nothing has to cross between parts.
Inputs may be any that keep to these rules, and one draw needn't show every extreme that they name: `near_lists`: slot 0 of row t names t itself; the following slots name leaves within 4 of t; after the named slots (at least 2) the row holds -1; all leaves of one device name equally many, some device names all 6 and some only 2. `cluster_lists`: row n names clusters within 4 of n, slot 0 names n itself. `upper_lists`: rows of level l (l = 1 to 3, 16 >> l rows each) follow those of lower levels; the row of node n names nodes of the same level within 4 of n, slot 0 names n itself. `positions`: atoms of leaf t have first coordinate within 4 of 2 t and the others within 4 of 0.
All inputs are finite; a program needn't handle non-finite values.
Results may differ from a plain program's by a relative error of at most 0.0057.
Values may be sent and summed in bfloat16 or wider, within the bound.
A program may use at most 128 MiB of HBM per device.

v0:
```python
import jax
import jax.numpy as jnp
from jax import lax
from jax.sharding import PartitionSpec as P

REACH = 4
CREACH = 4
UP = 3


SOFTEN = 1.0
HIGH = lax.Precision.HIGHEST


def padded(value, sides, width):
    for axis, dim in sides:
        peers, length = (lax.axis_size(axis), value.shape[dim])
        up = [(i, (i + 1) % peers) for i in range(peers - 1)]
        down = [(j, i) for i, j in up]
        last = lax.slice_in_dim(value, length - width, length, axis=dim)
        initial = lax.slice_in_dim(value, 0, width, axis=dim)
        before = lax.ppermute(last, axis, up)
        after = lax.ppermute(initial, axis, down)
        value = jnp.concatenate([before, value, after], axis=dim)
    return value


def from_partner(value, axis, stride):
    return lax.ppermute(value, axis, [(i, i ^ 1 << stride) for i in range(lax.axis_size(axis))])


def passed_along(block, axis, distance):
    devices = range(lax.axis_size(axis))
    route = [(i - distance, i) for i in devices if i - distance in devices]
    return lax.ppermute(block, axis, route)


def dipole_block(target_pos, source_pos):
    leaf_size = target_pos.shape[1]
    between = target_pos[:, :, None] - source_pos[:, None, :]
    radius = jnp.sum(between * between, axis=0) + SOFTEN * SOFTEN
    weight = 1.0 / radius
    falloff = weight * jnp.sqrt(weight)
    outer_part = (
        3.0
        * between[:, :, None, :]
        * jnp.transpose(between, (1, 0, 2))[None, :, :, :]
        * (weight * falloff)[None, :, None, :]
    )
    diagonal_part = jnp.eye(3, dtype=jnp.float32)[:, None, :, None] * falloff[None, :, None, :]
    return (outer_part - diagonal_part).reshape(3 * leaf_size, 3 * leaf_size).astype(jnp.bfloat16)


def apply_coupling(sources, coupling):
    return jnp.einsum("svl,skl->vk", sources, coupling.astype(jnp.float32), precision=HIGH)


def shards(
    probes,
    positions,
    polar,
    basis,
    leaf_transfer,
    cluster_transfer,
    upper_transfer,
    cluster_coupling,
    upper_coupling,
    near_lists,
    cluster_lists,
    upper_lists,
):
    local_leaves = probes.shape[0]
    vectors = probes.shape[1]
    leaf_size = probes.shape[3]
    rank = basis.shape[1]
    devices = lax.axis_size(("gx", "gy"))
    device = lax.axis_index(("gx", "gy"))
    root = jnp.sqrt(polar)
    scaled = (root[:, None, None, :] * probes.astype(jnp.float32)).astype(jnp.bfloat16)
    flat = scaled.reshape(local_leaves, vectors, 3 * leaf_size)
    basis_flat = basis.reshape(local_leaves, rank, 3 * leaf_size)
    wide_scaled = padded(scaled, ((("gx", "gy"), 0),), REACH)
    wide_sites = padded(positions, ((("gx", "gy"), 0),), REACH)
    wide_flat = wide_scaled.reshape(wide_scaled.shape[0], vectors, 3 * leaf_size)
    first_leaf = device * local_leaves - REACH

    def one_leaf(index, near_out):
        target = lax.dynamic_index_in_dim(positions, index, 0, keepdims=False)
        total = jnp.zeros((vectors, 3 * leaf_size), jnp.float32)
        for slot_index in range(near_lists.shape[1]):
            source = near_lists[index, slot_index]
            place = source - first_leaf

            def live_term(running):
                block = dipole_block(
                    target, lax.dynamic_index_in_dim(wide_sites, place, 0, keepdims=False)
                )
                rows_here = lax.dynamic_index_in_dim(wide_flat, place, 0, keepdims=False)
                return running + jnp.dot(rows_here, block.T, preferred_element_type=jnp.float32)

            total = lax.cond(source >= 0, live_term, lambda running: running, total)
        return near_out.at[index].set(total)

    near = lax.fori_loop(
        0, local_leaves, one_leaf, jnp.zeros((local_leaves, vectors, 3 * leaf_size), jnp.float32)
    )
    leaf_coef = lax.dot_general(
        flat, basis_flat, (((2,), (2,)), ((0,), (0,))), preferred_element_type=jnp.float32
    )
    carried = jnp.einsum(
        "tvl,tlk->tvk", leaf_coef, leaf_transfer.astype(jnp.float32), precision=HIGH
    )
    cluster = jnp.sum(carried, axis=0)
    lifted = jnp.einsum(
        "vl,lk->vk", cluster, cluster_transfer[0].astype(jnp.float32), precision=HIGH
    )

    def level_start(level_index):
        return devices - (devices >> level_index - 1)

    def level_rows(level_index):
        node = device >> level_index
        if level_index == 0:
            return (cluster_lists[0], cluster_coupling[0], node)
        place = level_start(level_index) + node
        return (
            lax.dynamic_index_in_dim(upper_lists, place, 0, keepdims=False),
            lax.dynamic_index_in_dim(upper_coupling, place, 0, keepdims=False),
            node,
        )

    fields = []
    coefs = [cluster]
    contrib = lifted
    for level_index in range(1, UP + 1):
        partner = from_partner(contrib, ("gx", "gy"), level_index - 1)
        current = contrib + partner
        coefs.append(current)
        if level_index < UP:
            upper_part = lax.dynamic_index_in_dim(
                upper_transfer,
                level_start(level_index) + (device >> level_index),
                0,
                keepdims=False,
            )
            contrib = jnp.einsum(
                "vl,lk->vk", current, upper_part.astype(jnp.float32), precision=HIGH
            )
    for level_index in range(UP + 1):
        stride = 1 << level_index
        candidates = []
        for offset in range(-CREACH, CREACH + 1):
            shift_by = -offset * stride
            if offset == 0:
                candidates.append(coefs[level_index])
            elif abs(shift_by) < devices:
                candidates.append(passed_along(coefs[level_index], ("gx", "gy"), shift_by))
            else:
                candidates.append(jnp.zeros_like(coefs[level_index]))
        stacked = jnp.stack(candidates, axis=0)
        lists_row, coupling_row, node = level_rows(level_index)
        offsets = jnp.arange(-CREACH, CREACH + 1, dtype=jnp.int32)
        chooser = (lists_row[:, None] - node == offsets[None, :]).astype(jnp.float32)
        sources = jnp.einsum("sm,mvk->svk", chooser, stacked, precision=HIGH)
        fields.append(apply_coupling(sources, coupling_row))
    down = fields[UP]
    for level_index in range(UP - 1, -1, -1):
        if level_index == 0:
            upper_part = cluster_transfer[0]
        else:
            upper_part = lax.dynamic_index_in_dim(
                upper_transfer,
                level_start(level_index) + (device >> level_index),
                0,
                keepdims=False,
            )
        down = fields[level_index] + jnp.einsum(
            "vk,lk->vl", down, upper_part.astype(jnp.float32), precision=HIGH
        )
    leaf_field = jnp.einsum(
        "vk,tlk->tvl", down, leaf_transfer.astype(jnp.float32), precision=HIGH
    ).astype(jnp.bfloat16)
    far = lax.dot_general(
        leaf_field, basis_flat, (((2,), (1,)), ((0,), (0,))), preferred_element_type=jnp.float32
    )
    total = (near + far).reshape(local_leaves, vectors, 3, leaf_size)
    return (total * root[:, None, None, :]).astype(jnp.bfloat16)


def solution(mesh):
    in_specs = (
        P(("groups", "gx", "gy"), None, None, None),
        P(("groups", "gx", "gy"), None, None),
        P(("groups", "gx", "gy"), None),
        P(("groups", "gx", "gy"), None, None, None),
        P(("groups", "gx", "gy"), None, None),
        P(("groups", "gx", "gy"), None, None),
        P("groups", None, None),
        P(("groups", "gx", "gy"), None, None, None),
        P("groups", None, None, None),
        P(("groups", "gx", "gy"), None),
        P(("groups", "gx", "gy"), None),
        P("groups", None),
    )
    out_specs = P(("groups", "gx", "gy"), None, None, None)
    return jax.shard_map(shards, mesh=mesh, in_specs=in_specs, out_specs=out_specs, check_vma=False)
```

profile of v0, /device:TPU:0, one launch (start us, length us, event | category | flops | bytes accessed | tf_op | source)
XLA Modules:
  0.0 592.0 jit_solution(3878486664812857418)
XLA Ops:
  164.4 425.9 %while.14 = (s32[]{:T(128)}, f32[4,16,1536]{2,1,0:T(8,128)S(1)}, s32[4,6]{1,0:T(4,128)S(1)}, s32[]{:T(128)}, f32[4,3,512]{2,0,1:T(4,128)}, /*index=5*/bf16[12,16...) while((s32[]{:T(128)}, f32[4,16,1536]{2,1,0:T(8,128)S(1)}, ...), condition=%wide.region_20.21_spmd, body=%wide.region_0.20_spmd.sunk | while | flops 552222912 | bytes 228484464 | solution.py:104
  192.8 15.6 %conditional.12 = (f32[16,1536]{1,0:T(8,128)S(1)}) conditional(s32[]{:T(128)} %convert_element_type.221, () %tuple.114, (s32[]{:T(128)}, bf16[12,16,1536]{2,1,0:T(8,128)(2,1)S(1)}, f32[3,512]{0,1:T(8,128)S(1)}, f32[12,3,512]{2,1,0:T(4,128)S(1)}, s32[]{:T(128)}) %tuple.137), branch_computations={%region_2.2_spmd, %region_3.0_spmd} | conditional | flops 92012568 | bytes 37945480 | solution.py:101
  195.2 9.9 %subtract_convert_fusion = bf16[3,512,3,512]{3,2,1,0:T(4,128)(2,1)S(1)} fusion(f32[512,512]{1,0:T(8,128)S(1)} %get-tuple-element.339, f32[3,3]{1,0:T(4,128)S(1)} %fusion.5, f32[512,512]{1,0:T(8,128)S(1)} %get-tuple-element.338, f32[512,3,512]{2,1,0:T(4,128)S(1)} %broadcast_subtract_fusion, f32[3,512,512]{2,1,0:T(8,128)S(1)} %get-tuple-element.340), kind=kLoop, calls=%fused_computation | loop fusion | flops 11796480 | bytes 13107236 | tf_op jit(solution)/shard_map/while/body/eval_jaxpr/cond/branch_1_fun/convert_element_type | solution.py:51
  208.4 15.6 %conditional.13 = (f32[16,1536]{1,0:T(8,128)S(1)}) conditional(s32[]{:T(128)} %convert_element_type.220, f32[16,1536]{1,0:T(8,128)S(1)} %get-tuple-element.466, (s32[]{:T(128)}, bf16[12,16,1536]{2,1,0:T(8,128)(2,1)S(1)}, f32[3,512]{0,1:T(8,128)S(1)}, f32[12,3,512]{2,1,0:T(4,128)S(1)}, f32[16,1536]{1,0:T(8,128)S(1)}, /*index=5*/s32[]{:T(128)}) %tuple.138), branch_computations={%region_5.5_spmd, %region_6.7_spmd} | conditional | flops 92037144 | bytes 38043784 | solution.py:101
  210.8 9.9 %subtract_convert_fusion.1 = bf16[3,512,3,512]{3,2,1,0:T(4,128)(2,1)S(1)} fusion(f32[512,512]{1,0:T(8,128)S(1)} %get-tuple-element.343, f32[3,3]{1,0:T(4,128)S(1)} %fusion.11, f32[512,512]{1,0:T(8,128)S(1)} %get-tuple-element.342, f32[512,3,512]{2,1,0:T(4,128)S(1)} %broadcast_subtract_fusion.1, f32[3,512,512]{2,1,0:T(8,128)S(1)} %get-tuple-element.344), kind=kLoop, calls=%fused_computation.15 | loop fusion | flops 11796480 | bytes 13107236 | tf_op jit(solution)/shard_map/while/body/eval_jaxpr/cond/branch_1_fun/convert_element_type | solution.py:51
  224.0 15.6 %conditional.14 = (f32[16,1536]{1,0:T(8,128)S(1)}) conditional(s32[]{:T(128)} %convert_element_type.219, f32[16,1536]{1,0:T(8,128)S(1)} %get-tuple-element.467, (s32[]{:T(128)}, bf16[12,16,1536]{2,1,0:T(8,128)(2,1)S(1)}, f32[3,512]{0,1:T(8,128)S(1)}, f32[12,3,512]{2,1,0:T(4,128)S(1)}, f32[16,1536]{1,0:T(8,128)S(1)}, /*index=5*/s32[]{:T(128)}) %tuple.139), branch_computations={%region_8.8_spmd, %region_9.10_spmd} | conditional | flops 92037144 | bytes 38043784 | solution.py:101
  226.4 9.9 %subtract_convert_fusion.2 = bf16[3,512,3,512]{3,2,1,0:T(4,128)(2,1)S(1)} fusion(f32[512,512]{1,0:T(8,128)S(1)} %get-tuple-element.347, f32[3,3]{1,0:T(4,128)S(1)} %fusion.17, f32[512,512]{1,0:T(8,128)S(1)} %get-tuple-element.346, f32[512,3,512]{2,1,0:T(4,128)S(1)} %broadcast_subtract_fusion.2, f32[3,512,512]{2,1,0:T(8,128)S(1)} %get-tuple-element.348), kind=kLoop, calls=%fused_computation.30 | loop fusion | flops 11796480 | bytes 13107236 | tf_op jit(solution)/shard_map/while/body/eval_jaxpr/cond/branch_1_fun/convert_element_type | solution.py:51
  239.6 15.6 %conditional.15 = (f32[16,1536]{1,0:T(8,128)S(1)}) conditional(s32[]{:T(128)} %convert_element_type.218, f32[16,1536]{1,0:T(8,128)S(1)} %get-tuple-element.468, (s32[]{:T(128)}, bf16[12,16,1536]{2,1,0:T(8,128)(2,1)S(1)}, f32[3,512]{0,1:T(8,128)S(1)}, f32[12,3,512]{2,1,0:T(4,128)S(1)}, f32[16,1536]{1,0:T(8,128)S(1)}, /*index=5*/s32[]{:T(128)}) %tuple.140), branch_computations={%region_11.11_spmd, %region_12.13_spmd} | conditional | flops 92037144 | bytes 38043784 | solution.py:101
  242.1 9.9 %subtract_convert_fusion.3 = bf16[3,512,3,512]{3,2,1,0:T(4,128)(2,1)S(1)} fusion(f32[512,512]{1,0:T(8,128)S(1)} %get-tuple-element.351, f32[3,3]{1,0:T(4,128)S(1)} %fusion.23, f32[512,512]{1,0:T(8,128)S(1)} %get-tuple-element.350, f32[512,3,512]{2,1,0:T(4,128)S(1)} %broadcast_subtract_fusion.3, f32[3,512,512]{2,1,0:T(8,128)S(1)} %get-tuple-element.352), kind=kLoop, calls=%fused_computation.45 | loop fusion | flops 11796480 | bytes 13107236 | tf_op jit(solution)/shard_map/while/body/eval_jaxpr/cond/branch_1_fun/convert_element_type | solution.py:51
  255.2 15.6 %conditional.16 = (f32[16,1536]{1,0:T(8,128)S(1)}) conditional(s32[]{:T(128)} %convert_element_type.217, f32[16,1536]{1,0:T(8,128)S(1)} %get-tuple-element.469, (s32[]{:T(128)}, bf16[12,16,1536]{2,1,0:T(8,128)(2,1)S(1)}, f32[3,512]{0,1:T(8,128)S(1)}, f32[12,3,512]{2,1,0:T(4,128)S(1)}, f32[16,1536]{1,0:T(8,128)S(1)}, /*index=5*/s32[]{:T(128)}) %tuple.141), branch_computations={%region_14.14_spmd, %region_15.16_spmd} | conditional | flops 92037144 | bytes 38043784 | solution.py:101
  257.7 9.9 %subtract_convert_fusion.4 = bf16[3,512,3,512]{3,2,1,0:T(4,128)(2,1)S(1)} fusion(f32[512,512]{1,0:T(8,128)S(1)} %get-tuple-element.355, f32[3,3]{1,0:T(4,128)S(1)} %fusion.29, f32[512,512]{1,0:T(8,128)S(1)} %get-tuple-element.354, f32[512,3,512]{2,1,0:T(4,128)S(1)} %broadcast_subtract_fusion.4, f32[3,512,512]{2,1,0:T(8,128)S(1)} %get-tuple-element.356), kind=kLoop, calls=%fused_computation.60 | loop fusion | flops 11796480 | bytes 13107236 | tf_op jit(solution)/shard_map/while/body/eval_jaxpr/cond/branch_1_fun/convert_element_type | solution.py:51
  270.9 15.7 %conditional.17 = (f32[1,16,1536]{2,1,0:T(8,128)S(1)}) conditional(s32[]{:T(128)} %convert_element_type.216, f32[16,1536]{1,0:T(8,128)S(1)} %get-tuple-element.470, (s32[]{:T(128)}, s32[]{:T(128)}, bf16[12,16,1536]{2,1,0:T(8,128)(2,1)S(1)}, f32[3,512]{0,1:T(8,128)S(1)}, f32[12,3,512]{2,1,0:T(4,128)S(1)}, ...), branch_computations={%region_17.17_spmd, %region_18.19_spmd} | conditional | flops 92037144 | bytes 38043784 | solution.py:101
  273.4 9.9 %subtract_convert_fusion.5 = bf16[3,512,3,512]{3,2,1,0:T(4,128)(2,1)S(1)} fusion(f32[512,512]{1,0:T(8,128)S(1)} %get-tuple-element.359, f32[3,3]{1,0:T(4,128)S(1)} %fusion.36, f32[512,512]{1,0:T(8,128)S(1)} %get-tuple-element.358, f32[512,3,512]{2,1,0:T(4,128)S(1)} %broadcast_subtract_fusion.5, f32[3,512,512]{2,1,0:T(8,128)S(1)} %get-tuple-element.360), kind=kLoop, calls=%fused_computation.75 | loop fusion | flops 11796480 | bytes 13107236 | tf_op jit(solution)/shard_map/while/body/eval_jaxpr/cond/branch_1_fun/convert_element_type | solution.py:51
  293.5 15.6 %conditional.12 = (f32[16,1536]{1,0:T(8,128)S(1)}) conditional(s32[]{:T(128)} %convert_element_type.221, () %tuple.114, (s32[]{:T(128)}, bf16[12,16,1536]{2,1,0:T(8,128)(2,1)S(1)}, f32[3,512]{0,1:T(8,128)S(1)}, f32[12,3,512]{2,1,0:T(4,128)S(1)}, s32[]{:T(128)}) %tuple.137), branch_computations={%region_2.2_spmd, %region_3.0_spmd} | conditional | flops 92012568 | bytes 37945480 | solution.py:101
  295.9 9.9 %subtract_convert_fusion = bf16[3,512,3,512]{3,2,1,0:T(4,128)(2,1)S(1)} fusion(f32[512,512]{1,0:T(8,128)S(1)} %get-tuple-element.339, f32[3,3]{1,0:T(4,128)S(1)} %fusion.5, f32[512,512]{1,0:T(8,128)S(1)} %get-tuple-element.338, f32[512,3,512]{2,1,0:T(4,128)S(1)} %broadcast_subtract_fusion, f32[3,512,512]{2,1,0:T(8,128)S(1)} %get-tuple-element.340), kind=kLoop, calls=%fused_computation | loop fusion | flops 11796480 | bytes 13107236 | tf_op jit(solution)/shard_map/while/body/eval_jaxpr/cond/branch_1_fun/convert_element_type | solution.py:51
  309.1 15.6 %conditional.13 = (f32[16,1536]{1,0:T(8,128)S(1)}) conditional(s32[]{:T(128)} %convert_element_type.220, f32[16,1536]{1,0:T(8,128)S(1)} %get-tuple-element.466, (s32[]{:T(128)}, bf16[12,16,1536]{2,1,0:T(8,128)(2,1)S(1)}, f32[3,512]{0,1:T(8,128)S(1)}, f32[12,3,512]{2,1,0:T(4,128)S(1)}, f32[16,1536]{1,0:T(8,128)S(1)}, /*index=5*/s32[]{:T(128)}) %tuple.138), branch_computations={%region_5.5_spmd, %region_6.7_spmd} | conditional | flops 92037144 | bytes 38043784 | solution.py:101
  311.6 9.9 %subtract_convert_fusion.1 = bf16[3,512,3,512]{3,2,1,0:T(4,128)(2,1)S(1)} fusion(f32[512,512]{1,0:T(8,128)S(1)} %get-tuple-element.343, f32[3,3]{1,0:T(4,128)S(1)} %fusion.11, f32[512,512]{1,0:T(8,128)S(1)} %get-tuple-element.342, f32[512,3,512]{2,1,0:T(4,128)S(1)} %broadcast_subtract_fusion.1, f32[3,512,512]{2,1,0:T(8,128)S(1)} %get-tuple-element.344), kind=kLoop, calls=%fused_computation.15 | loop fusion | flops 11796480 | bytes 13107236 | tf_op jit(solution)/shard_map/while/body/eval_jaxpr/cond/branch_1_fun/convert_element_type | solution.py:51
  324.8 15.6 %conditional.14 = (f32[16,1536]{1,0:T(8,128)S(1)}) conditional(s32[]{:T(128)} %convert_element_type.219, f32[16,1536]{1,0:T(8,128)S(1)} %get-tuple-element.467, (s32[]{:T(128)}, bf16[12,16,1536]{2,1,0:T(8,128)(2,1)S(1)}, f32[3,512]{0,1:T(8,128)S(1)}, f32[12,3,512]{2,1,0:T(4,128)S(1)}, f32[16,1536]{1,0:T(8,128)S(1)}, /*index=5*/s32[]{:T(128)}) %tuple.139), branch_computations={%region_8.8_spmd, %region_9.10_spmd} | conditional | flops 92037144 | bytes 38043784 | solution.py:101
  327.1 9.9 %subtract_convert_fusion.2 = bf16[3,512,3,512]{3,2,1,0:T(4,128)(2,1)S(1)} fusion(f32[512,512]{1,0:T(8,128)S(1)} %get-tuple-element.347, f32[3,3]{1,0:T(4,128)S(1)} %fusion.17, f32[512,512]{1,0:T(8,128)S(1)} %get-tuple-element.346, f32[512,3,512]{2,1,0:T(4,128)S(1)} %broadcast_subtract_fusion.2, f32[3,512,512]{2,1,0:T(8,128)S(1)} %get-tuple-element.348), kind=kLoop, calls=%fused_computation.30 | loop fusion | flops 11796480 | bytes 13107236 | tf_op jit(solution)/shard_map/while/body/eval_jaxpr/cond/branch_1_fun/convert_element_type | solution.py:51
  340.3 15.6 %conditional.15 = (f32[16,1536]{1,0:T(8,128)S(1)}) conditional(s32[]{:T(128)} %convert_element_type.218, f32[16,1536]{1,0:T(8,128)S(1)} %get-tuple-element.468, (s32[]{:T(128)}, bf16[12,16,1536]{2,1,0:T(8,128)(2,1)S(1)}, f32[3,512]{0,1:T(8,128)S(1)}, f32[12,3,512]{2,1,0:T(4,128)S(1)}, f32[16,1536]{1,0:T(8,128)S(1)}, /*index=5*/s32[]{:T(128)}) %tuple.140), branch_computations={%region_11.11_spmd, %region_12.13_spmd} | conditional | flops 92037144 | bytes 38043784 | solution.py:101
  342.8 9.9 %subtract_convert_fusion.3 = bf16[3,512,3,512]{3,2,1,0:T(4,128)(2,1)S(1)} fusion(f32[512,512]{1,0:T(8,128)S(1)} %get-tuple-element.351, f32[3,3]{1,0:T(4,128)S(1)} %fusion.23, f32[512,512]{1,0:T(8,128)S(1)} %get-tuple-element.350, f32[512,3,512]{2,1,0:T(4,128)S(1)} %broadcast_subtract_fusion.3, f32[3,512,512]{2,1,0:T(8,128)S(1)} %get-tuple-element.352), kind=kLoop, calls=%fused_computation.45 | loop fusion | flops 11796480 | bytes 13107236 | tf_op jit(solution)/shard_map/while/body/eval_jaxpr/cond/branch_1_fun/convert_element_type | solution.py:51
  356.0 15.6 %conditional.16 = (f32[16,1536]{1,0:T(8,128)S(1)}) conditional(s32[]{:T(128)} %convert_element_type.217, f32[16,1536]{1,0:T(8,128)S(1)} %get-tuple-element.469, (s32[]{:T(128)}, bf16[12,16,1536]{2,1,0:T(8,128)(2,1)S(1)}, f32[3,512]{0,1:T(8,128)S(1)}, f32[12,3,512]{2,1,0:T(4,128)S(1)}, f32[16,1536]{1,0:T(8,128)S(1)}, /*index=5*/s32[]{:T(128)}) %tuple.141), branch_computations={%region_14.14_spmd, %region_15.16_spmd} | conditional | flops 92037144 | bytes 38043784 | solution.py:101
  358.4 9.9 %subtract_convert_fusion.4 = bf16[3,512,3,512]{3,2,1,0:T(4,128)(2,1)S(1)} fusion(f32[512,512]{1,0:T(8,128)S(1)} %get-tuple-element.355, f32[3,3]{1,0:T(4,128)S(1)} %fusion.29, f32[512,512]{1,0:T(8,128)S(1)} %get-tuple-element.354, f32[512,3,512]{2,1,0:T(4,128)S(1)} %broadcast_subtract_fusion.4, f32[3,512,512]{2,1,0:T(8,128)S(1)} %get-tuple-element.356), kind=kLoop, calls=%fused_computation.60 | loop fusion | flops 11796480 | bytes 13107236 | tf_op jit(solution)/shard_map/while/body/eval_jaxpr/cond/branch_1_fun/convert_element_type | solution.py:51
  371.6 15.7 %conditional.17 = (f32[1,16,1536]{2,1,0:T(8,128)S(1)}) conditional(s32[]{:T(128)} %convert_element_type.216, f32[16,1536]{1,0:T(8,128)S(1)} %get-tuple-element.470, (s32[]{:T(128)}, s32[]{:T(128)}, bf16[12,16,1536]{2,1,0:T(8,128)(2,1)S(1)}, f32[3,512]{0,1:T(8,128)S(1)}, f32[12,3,512]{2,1,0:T(4,128)S(1)}, ...), branch_computations={%region_17.17_spmd, %region_18.19_spmd} | conditional | flops 92037144 | bytes 38043784 | solution.py:101
  374.1 9.9 %subtract_convert_fusion.5 = bf16[3,512,3,512]{3,2,1,0:T(4,128)(2,1)S(1)} fusion(f32[512,512]{1,0:T(8,128)S(1)} %get-tuple-element.359, f32[3,3]{1,0:T(4,128)S(1)} %fusion.36, f32[512,512]{1,0:T(8,128)S(1)} %get-tuple-element.358, f32[512,3,512]{2,1,0:T(4,128)S(1)} %broadcast_subtract_fusion.5, f32[3,512,512]{2,1,0:T(8,128)S(1)} %get-tuple-element.360), kind=kLoop, calls=%fused_computation.75 | loop fusion | flops 11796480 | bytes 13107236 | tf_op jit(solution)/shard_map/while/body/eval_jaxpr/cond/branch_1_fun/convert_element_type | solution.py:51
  394.2 15.6 %conditional.12 = (f32[16,1536]{1,0:T(8,128)S(1)}) conditional(s32[]{:T(128)} %convert_element_type.221, () %tuple.114, (s32[]{:T(128)}, bf16[12,16,1536]{2,1,0:T(8,128)(2,1)S(1)}, f32[3,512]{0,1:T(8,128)S(1)}, f32[12,3,512]{2,1,0:T(4,128)S(1)}, s32[]{:T(128)}) %tuple.137), branch_computations={%region_2.2_spmd, %region_3.0_spmd} | conditional | flops 92012568 | bytes 37945480 | solution.py:101
  396.7 9.9 %subtract_convert_fusion = bf16[3,512,3,512]{3,2,1,0:T(4,128)(2,1)S(1)} fusion(f32[512,512]{1,0:T(8,128)S(1)} %get-tuple-element.339, f32[3,3]{1,0:T(4,128)S(1)} %fusion.5, f32[512,512]{1,0:T(8,128)S(1)} %get-tuple-element.338, f32[512,3,512]{2,1,0:T(4,128)S(1)} %broadcast_subtract_fusion, f32[3,512,512]{2,1,0:T(8,128)S(1)} %get-tuple-element.340), kind=kLoop, calls=%fused_computation | loop fusion | flops 11796480 | bytes 13107236 | tf_op jit(solution)/shard_map/while/body/eval_jaxpr/cond/branch_1_fun/convert_element_type | solution.py:51
  409.9 15.6 %conditional.13 = (f32[16,1536]{1,0:T(8,128)S(1)}) conditional(s32[]{:T(128)} %convert_element_type.220, f32[16,1536]{1,0:T(8,128)S(1)} %get-tuple-element.466, (s32[]{:T(128)}, bf16[12,16,1536]{2,1,0:T(8,128)(2,1)S(1)}, f32[3,512]{0,1:T(8,128)S(1)}, f32[12,3,512]{2,1,0:T(4,128)S(1)}, f32[16,1536]{1,0:T(8,128)S(1)}, /*index=5*/s32[]{:T(128)}) %tuple.138), branch_computations={%region_5.5_spmd, %region_6.7_spmd} | conditional | flops 92037144 | bytes 38043784 | solution.py:101
  412.3 9.9 %subtract_convert_fusion.1 = bf16[3,512,3,512]{3,2,1,0:T(4,128)(2,1)S(1)} fusion(f32[512,512]{1,0:T(8,128)S(1)} %get-tuple-element.343, f32[3,3]{1,0:T(4,128)S(1)} %fusion.11, f32[512,512]{1,0:T(8,128)S(1)} %get-tuple-element.342, f32[512,3,512]{2,1,0:T(4,128)S(1)} %broadcast_subtract_fusion.1, f32[3,512,512]{2,1,0:T(8,128)S(1)} %get-tuple-element.344), kind=kLoop, calls=%fused_computation.15 | loop fusion | flops 11796480 | bytes 13107236 | tf_op jit(solution)/shard_map/while/body/eval_jaxpr/cond/branch_1_fun/convert_element_type | solution.py:51
  425.5 15.6 %conditional.14 = (f32[16,1536]{1,0:T(8,128)S(1)}) conditional(s32[]{:T(128)} %convert_element_type.219, f32[16,1536]{1,0:T(8,128)S(1)} %get-tuple-element.467, (s32[]{:T(128)}, bf16[12,16,1536]{2,1,0:T(8,128)(2,1)S(1)}, f32[3,512]{0,1:T(8,128)S(1)}, f32[12,3,512]{2,1,0:T(4,128)S(1)}, f32[16,1536]{1,0:T(8,128)S(1)}, /*index=5*/s32[]{:T(128)}) %tuple.139), branch_computations={%region_8.8_spmd, %region_9.10_spmd} | conditional | flops 92037144 | bytes 38043784 | solution.py:101
  427.9 9.9 %subtract_convert_fusion.2 = bf16[3,512,3,512]{3,2,1,0:T(4,128)(2,1)S(1)} fusion(f32[512,512]{1,0:T(8,128)S(1)} %get-tuple-element.347, f32[3,3]{1,0:T(4,128)S(1)} %fusion.17, f32[512,512]{1,0:T(8,128)S(1)} %get-tuple-element.346, f32[512,3,512]{2,1,0:T(4,128)S(1)} %broadcast_subtract_fusion.2, f32[3,512,512]{2,1,0:T(8,128)S(1)} %get-tuple-element.348), kind=kLoop, calls=%fused_computation.30 | loop fusion | flops 11796480 | bytes 13107236 | tf_op jit(solution)/shard_map/while/body/eval_jaxpr/cond/branch_1_fun/convert_element_type | solution.py:51
  441.1 15.6 %conditional.15 = (f32[16,1536]{1,0:T(8,128)S(1)}) conditional(s32[]{:T(128)} %convert_element_type.218, f32[16,1536]{1,0:T(8,128)S(1)} %get-tuple-element.468, (s32[]{:T(128)}, bf16[12,16,1536]{2,1,0:T(8,128)(2,1)S(1)}, f32[3,512]{0,1:T(8,128)S(1)}, f32[12,3,512]{2,1,0:T(4,128)S(1)}, f32[16,1536]{1,0:T(8,128)S(1)}, /*index=5*/s32[]{:T(128)}) %tuple.140), branch_computations={%region_11.11_spmd, %region_12.13_spmd} | conditional | flops 92037144 | bytes 38043784 | solution.py:101
  443.5 9.9 %subtract_convert_fusion.3 = bf16[3,512,3,512]{3,2,1,0:T(4,128)(2,1)S(1)} fusion(f32[512,512]{1,0:T(8,128)S(1)} %get-tuple-element.351, f32[3,3]{1,0:T(4,128)S(1)} %fusion.23, f32[512,512]{1,0:T(8,128)S(1)} %get-tuple-element.350, f32[512,3,512]{2,1,0:T(4,128)S(1)} %broadcast_subtract_fusion.3, f32[3,512,512]{2,1,0:T(8,128)S(1)} %get-tuple-element.352), kind=kLoop, calls=%fused_computation.45 | loop fusion | flops 11796480 | bytes 13107236 | tf_op jit(solution)/shard_map/while/body/eval_jaxpr/cond/branch_1_fun/convert_element_type | solution.py:51
  456.7 15.6 %conditional.16 = (f32[16,1536]{1,0:T(8,128)S(1)}) conditional(s32[]{:T(128)} %convert_element_type.217, f32[16,1536]{1,0:T(8,128)S(1)} %get-tuple-element.469, (s32[]{:T(128)}, bf16[12,16,1536]{2,1,0:T(8,128)(2,1)S(1)}, f32[3,512]{0,1:T(8,128)S(1)}, f32[12,3,512]{2,1,0:T(4,128)S(1)}, f32[16,1536]{1,0:T(8,128)S(1)}, /*index=5*/s32[]{:T(128)}) %tuple.141), branch_computations={%region_14.14_spmd, %region_15.16_spmd} | conditional | flops 92037144 | bytes 38043784 | solution.py:101
  459.1 9.9 %subtract_convert_fusion.4 = bf16[3,512,3,512]{3,2,1,0:T(4,128)(2,1)S(1)} fusion(f32[512,512]{1,0:T(8,128)S(1)} %get-tuple-element.355, f32[3,3]{1,0:T(4,128)S(1)} %fusion.29, f32[512,512]{1,0:T(8,128)S(1)} %get-tuple-element.354, f32[512,3,512]{2,1,0:T(4,128)S(1)} %broadcast_subtract_fusion.4, f32[3,512,512]{2,1,0:T(8,128)S(1)} %get-tuple-element.356), kind=kLoop, calls=%fused_computation.60 | loop fusion | flops 11796480 | bytes 13107236 | tf_op jit(solution)/shard_map/while/body/eval_jaxpr/cond/branch_1_fun/convert_element_type | solution.py:51
  472.3 15.7 %conditional.17 = (f32[1,16,1536]{2,1,0:T(8,128)S(1)}) conditional(s32[]{:T(128)} %convert_element_type.216, f32[16,1536]{1,0:T(8,128)S(1)} %get-tuple-element.470, (s32[]{:T(128)}, s32[]{:T(128)}, bf16[12,16,1536]{2,1,0:T(8,128)(2,1)S(1)}, f32[3,512]{0,1:T(8,128)S(1)}, f32[12,3,512]{2,1,0:T(4,128)S(1)}, ...), branch_computations={%region_17.17_spmd, %region_18.19_spmd} | conditional | flops 92037144 | bytes 38043784 | solution.py:101
  474.8 9.9 %subtract_convert_fusion.5 = bf16[3,512,3,512]{3,2,1,0:T(4,128)(2,1)S(1)} fusion(f32[512,512]{1,0:T(8,128)S(1)} %get-tuple-element.359, f32[3,3]{1,0:T(4,128)S(1)} %fusion.36, f32[512,512]{1,0:T(8,128)S(1)} %get-tuple-element.358, f32[512,3,512]{2,1,0:T(4,128)S(1)} %broadcast_subtract_fusion.5, f32[3,512,512]{2,1,0:T(8,128)S(1)} %get-tuple-element.360), kind=kLoop, calls=%fused_computation.75 | loop fusion | flops 11796480 | bytes 13107236 | tf_op jit(solution)/shard_map/while/body/eval_jaxpr/cond/branch_1_fun/convert_element_type | solution.py:51
  494.9 15.6 %conditional.12 = (f32[16,1536]{1,0:T(8,128)S(1)}) conditional(s32[]{:T(128)} %convert_element_type.221, () %tuple.114, (s32[]{:T(128)}, bf16[12,16,1536]{2,1,0:T(8,128)(2,1)S(1)}, f32[3,512]{0,1:T(8,128)S(1)}, f32[12,3,512]{2,1,0:T(4,128)S(1)}, s32[]{:T(128)}) %tuple.137), branch_computations={%region_2.2_spmd, %region_3.0_spmd} | conditional | flops 92012568 | bytes 37945480 | solution.py:101
  497.4 9.9 %subtract_convert_fusion = bf16[3,512,3,512]{3,2,1,0:T(4,128)(2,1)S(1)} fusion(f32[512,512]{1,0:T(8,128)S(1)} %get-tuple-element.339, f32[3,3]{1,0:T(4,128)S(1)} %fusion.5, f32[512,512]{1,0:T(8,128)S(1)} %get-tuple-element.338, f32[512,3,512]{2,1,0:T(4,128)S(1)} %broadcast_subtract_fusion, f32[3,512,512]{2,1,0:T(8,128)S(1)} %get-tuple-element.340), kind=kLoop, calls=%fused_computation | loop fusion | flops 11796480 | bytes 13107236 | tf_op jit(solution)/shard_map/while/body/eval_jaxpr/cond/branch_1_fun/convert_element_type | solution.py:51
  510.6 15.6 %conditional.13 = (f32[16,1536]{1,0:T(8,128)S(1)}) conditional(s32[]{:T(128)} %convert_element_type.220, f32[16,1536]{1,0:T(8,128)S(1)} %get-tuple-element.466, (s32[]{:T(128)}, bf16[12,16,1536]{2,1,0:T(8,128)(2,1)S(1)}, f32[3,512]{0,1:T(8,128)S(1)}, f32[12,3,512]{2,1,0:T(4,128)S(1)}, f32[16,1536]{1,0:T(8,128)S(1)}, /*index=5*/s32[]{:T(128)}) %tuple.138), branch_computations={%region_5.5_spmd, %region_6.7_spmd} | conditional | flops 92037144 | bytes 38043784 | solution.py:101
  513.0 9.9 %subtract_convert_fusion.1 = bf16[3,512,3,512]{3,2,1,0:T(4,128)(2,1)S(1)} fusion(f32[512,512]{1,0:T(8,128)S(1)} %get-tuple-element.343, f32[3,3]{1,0:T(4,128)S(1)} %fusion.11, f32[512,512]{1,0:T(8,128)S(1)} %get-tuple-element.342, f32[512,3,512]{2,1,0:T(4,128)S(1)} %broadcast_subtract_fusion.1, f32[3,512,512]{2,1,0:T(8,128)S(1)} %get-tuple-element.344), kind=kLoop, calls=%fused_computation.15 | loop fusion | flops 11796480 | bytes 13107236 | tf_op jit(solution)/shard_map/while/body/eval_jaxpr/cond/branch_1_fun/convert_element_type | solution.py:51
  526.2 15.6 %conditional.14 = (f32[16,1536]{1,0:T(8,128)S(1)}) conditional(s32[]{:T(128)} %convert_element_type.219, f32[16,1536]{1,0:T(8,128)S(1)} %get-tuple-element.467, (s32[]{:T(128)}, bf16[12,16,1536]{2,1,0:T(8,128)(2,1)S(1)}, f32[3,512]{0,1:T(8,128)S(1)}, f32[12,3,512]{2,1,0:T(4,128)S(1)}, f32[16,1536]{1,0:T(8,128)S(1)}, /*index=5*/s32[]{:T(128)}) %tuple.139), branch_computations={%region_8.8_spmd, %region_9.10_spmd} | conditional | flops 92037144 | bytes 38043784 | solution.py:101
  528.6 9.9 %subtract_convert_fusion.2 = bf16[3,512,3,512]{3,2,1,0:T(4,128)(2,1)S(1)} fusion(f32[512,512]{1,0:T(8,128)S(1)} %get-tuple-element.347, f32[3,3]{1,0:T(4,128)S(1)} %fusion.17, f32[512,512]{1,0:T(8,128)S(1)} %get-tuple-element.346, f32[512,3,512]{2,1,0:T(4,128)S(1)} %broadcast_subtract_fusion.2, f32[3,512,512]{2,1,0:T(8,128)S(1)} %get-tuple-element.348), kind=kLoop, calls=%fused_computation.30 | loop fusion | flops 11796480 | bytes 13107236 | tf_op jit(solution)/shard_map/while/body/eval_jaxpr/cond/branch_1_fun/convert_element_type | solution.py:51
  541.8 15.6 %conditional.15 = (f32[16,1536]{1,0:T(8,128)S(1)}) conditional(s32[]{:T(128)} %convert_element_type.218, f32[16,1536]{1,0:T(8,128)S(1)} %get-tuple-element.468, (s32[]{:T(128)}, bf16[12,16,1536]{2,1,0:T(8,128)(2,1)S(1)}, f32[3,512]{0,1:T(8,128)S(1)}, f32[12,3,512]{2,1,0:T(4,128)S(1)}, f32[16,1536]{1,0:T(8,128)S(1)}, /*index=5*/s32[]{:T(128)}) %tuple.140), branch_computations={%region_11.11_spmd, %region_12.13_spmd} | conditional | flops 92037144 | bytes 38043784 | solution.py:101
  557.4 15.6 %conditional.16 = (f32[16,1536]{1,0:T(8,128)S(1)}) conditional(s32[]{:T(128)} %convert_element_type.217, f32[16,1536]{1,0:T(8,128)S(1)} %get-tuple-element.469, (s32[]{:T(128)}, bf16[12,16,1536]{2,1,0:T(8,128)(2,1)S(1)}, f32[3,512]{0,1:T(8,128)S(1)}, f32[12,3,512]{2,1,0:T(4,128)S(1)}, f32[16,1536]{1,0:T(8,128)S(1)}, /*index=5*/s32[]{:T(128)}) %tuple.141), branch_computations={%region_14.14_spmd, %region_15.16_spmd} | conditional | flops 92037144 | bytes 38043784 | solution.py:101
  559.9 9.9 %subtract_convert_fusion.4 = bf16[3,512,3,512]{3,2,1,0:T(4,128)(2,1)S(1)} fusion(f32[512,512]{1,0:T(8,128)S(1)} %get-tuple-element.355, f32[3,3]{1,0:T(4,128)S(1)} %fusion.29, f32[512,512]{1,0:T(8,128)S(1)} %get-tuple-element.354, f32[512,3,512]{2,1,0:T(4,128)S(1)} %broadcast_subtract_fusion.4, f32[3,512,512]{2,1,0:T(8,128)S(1)} %get-tuple-element.356), kind=kLoop, calls=%fused_computation.60 | loop fusion | flops 11796480 | bytes 13107236 | tf_op jit(solution)/shard_map/while/body/eval_jaxpr/cond/branch_1_fun/convert_element_type | solution.py:51
  573.1 15.7 %conditional.17 = (f32[1,16,1536]{2,1,0:T(8,128)S(1)}) conditional(s32[]{:T(128)} %convert_element_type.216, f32[16,1536]{1,0:T(8,128)S(1)} %get-tuple-element.470, (s32[]{:T(128)}, s32[]{:T(128)}, bf16[12,16,1536]{2,1,0:T(8,128)(2,1)S(1)}, f32[3,512]{0,1:T(8,128)S(1)}, f32[12,3,512]{2,1,0:T(4,128)S(1)}, ...), branch_computations={%region_17.17_spmd, %region_18.19_spmd} | conditional | flops 92037144 | bytes 38043784 | solution.py:101
  575.6 9.9 %subtract_convert_fusion.5 = bf16[3,512,3,512]{3,2,1,0:T(4,128)(2,1)S(1)} fusion(f32[512,512]{1,0:T(8,128)S(1)} %get-tuple-element.359, f32[3,3]{1,0:T(4,128)S(1)} %fusion.36, f32[512,512]{1,0:T(8,128)S(1)} %get-tuple-element.358, f32[512,3,512]{2,1,0:T(4,128)S(1)} %broadcast_subtract_fusion.5, f32[3,512,512]{2,1,0:T(8,128)S(1)} %get-tuple-element.360), kind=kLoop, calls=%fused_computation.75 | loop fusion | flops 11796480 | bytes 13107236 | tf_op jit(solution)/shard_map/while/body/eval_jaxpr/cond/branch_1_fun/convert_element_type | solution.py:51
  (364 shorter events, 308.8 us)
Async XLA Ops:
  0.0 127.7 %copy-start = (bf16[14,6,64,64]{3,2,1,0:T(8,128)(2,1)S(1)}, bf16[14,6,64,64]{3,2,1,0:T(8,128)(2,1)}, u32[]{:S(2)}) copy-start(bf16[14,6,64,64]{3,2,1,0:T(8,128)(2,1)} %param.36) | copy-start | bytes 2064388
  0.0 161.5 %copy-start.3 = (bf16[4,64,64]{2,1,0:T(8,128)(2,1)S(1)}, bf16[4,64,64]{2,1,0:T(8,128)(2,1)}, u32[]{:S(2)}) copy-start(bf16[4,64,64]{2,1,0:T(8,128)(2,1)} %param.32) | copy-start | bytes 98308
  0.0 161.4 %copy-start.7 = (bf16[1,64,64]{2,1,0:T(8,128)(2,1)S(1)}, bf16[1,64,64]{2,1,0:T(8,128)(2,1)}, u32[]{:S(2)}) copy-start(bf16[1,64,64]{2,1,0:T(8,128)(2,1)} %param.33) | copy-start | bytes 24580
  0.8 10.1 %copy-start.5 = (f32[4,512]{1,0:T(4,128)}, f32[4,512]{1,0:T(4,128)S(1)}, u32[]{:S(2)}) copy-start(f32[4,512]{1,0:T(4,128)S(1)} %sqrt.63) | copy-start | bytes 24580
  2.0 160.9 %collective-permute-start.1 = (bf16[4,16,3,512]{3,2,1,0:T(4,128)(2,1)S(1)}, bf16[4,16,3,512]{3,2,1,0:T(4,128)(2,1)S(1)}, u32[]{:S(2)}, u32[]{:S(2)}) collective-permute-start(bf16[4,16,3,512]{3,2,1,0:T(4,128)(2,1)S(1)} %multiply_convert_fusion.1), channel_id=1, source_target_pairs={{1,0},{2,1},{3,2},{4,3},{5,4},{6,5},{7,6},{8,7},{9,8},{10,9},{11,1... | collective-permute-start | bytes 589832 | tf_op jit(solution)/shard_map/ppermute | solution.py:23
  3.3 159.6 %collective-permute-start = (bf16[4,16,3,512]{3,2,1,0:T(4,128)(2,1)S(1)}, bf16[4,16,3,512]{3,2,1,0:T(4,128)(2,1)S(1)}, u32[]{:S(2)}, u32[]{:S(2)}) collective-permute-start(bf16[4,16,3,512]{3,2,1,0:T(4,128)(2,1)S(1)} %multiply_convert_fusion.1), channel_id=1, source_target_pairs={{0,1},{1,2},{2,3},{3,4},{4,5},{5,6},{6,7},{7,8},{8,9},{9,10},{10,1... | collective-permute-start | bytes 589832 | tf_op jit(solution)/shard_map/ppermute | solution.py:22
  9.6 153.3 %collective-permute-start.3 = (f32[4,3,512]{2,1,0:T(4,128)S(1)}, f32[4,3,512]{2,1,0:T(4,128)S(1)}, u32[]{:S(2)}, u32[]{:S(2)}) collective-permute-start(f32[4,3,512]{2,1,0:T(4,128)S(1)} %copy.31), channel_id=1, source_target_pairs={{1,0},{2,1},{3,2},{4,3},{5,4},{6,5},{7,6},{8,7},{9,8},{10,9},{11,1... | collective-permute-start | bytes 73736 | tf_op jit(solution)/shard_map/ppermute | solution.py:23
  10.9 151.9 %collective-permute-start.2 = (f32[4,3,512]{2,1,0:T(4,128)S(1)}, f32[4,3,512]{2,1,0:T(4,128)S(1)}, u32[]{:S(2)}, u32[]{:S(2)}) collective-permute-start(f32[4,3,512]{2,1,0:T(4,128)S(1)} %copy.31), channel_id=1, source_target_pairs={{0,1},{1,2},{2,3},{3,4},{4,5},{5,6},{6,7},{7,8},{8,9},{9,10},{10,1... | collective-permute-start | bytes 73736 | tf_op jit(solution)/shard_map/ppermute | solution.py:22
  15.7 148.6 %copy-start.4 = (s32[4,6]{1,0:T(4,128)S(1)}, s32[4,6]{1,0:T(4,128)}, u32[]{:S(2)}) copy-start(s32[4,6]{1,0:T(4,128)} %param.37) | copy-start | bytes 292
  15.7 148.6 %copy-start.8 = (s32[3]{0:T(128)S(1)}, s32[3]{0:T(128)}, u32[]{:S(2)}) copy-start(s32[3]{0:T(128)} %constant.206.clone.1) | copy-start | bytes 40
  18.3 8.1 %collective-permute-start.4 = (f32[16,64]{1,0:T(8,128)S(1)}, f32[16,64]{1,0:T(8,128)S(1)}, u32[]{:S(2)}, u32[]{:S(2)}) collective-permute-start(f32[16,64]{1,0:T(8,128)S(1)} %bitcast.242), channel_id=1, source_target_pairs={{0,4},{1,5},{2,6},{3,7},{4,8},{5,9},{6,10},{7,11},{8,12},{9,13},{1... | collective-permute-start | bytes 12296 | tf_op jit(solution)/shard_map/ppermute | solution.py:35
  26.5 8.3 %collective-permute-start.5 = (f32[16,64]{1,0:T(8,128)S(1)}, f32[16,64]{1,0:T(8,128)S(1)}, u32[]{:S(2)}, u32[]{:S(2)}) collective-permute-start(f32[16,64]{1,0:T(8,128)S(1)} %bitcast.243), channel_id=1, source_target_pairs={{0,3},{1,4},{2,5},{3,6},{4,7},{5,8},{6,9},{7,10},{8,11},{9,12},{10... | collective-permute-start | bytes 12296 | tf_op jit(solution)/shard_map/ppermute | solution.py:35
  34.8 2.6 collective-permute-start.6
  37.4 8.5 %collective-permute-start.7 = (f32[16,64]{1,0:T(8,128)S(1)}, f32[16,64]{1,0:T(8,128)S(1)}, u32[]{:S(2)}, u32[]{:S(2)}) collective-permute-start(f32[16,64]{1,0:T(8,128)S(1)} %bitcast.245), channel_id=1, source_target_pairs={{0,1},{1,2},{2,3},{3,4},{4,5},{5,6},{6,7},{7,8},{8,9},{9,10},{10,1... | collective-permute-start | bytes 12296 | tf_op jit(solution)/shard_map/ppermute | solution.py:35
  45.9 3.9 collective-permute-start.12
  49.8 5.5 collective-permute-start.8
  55.4 6.7 %collective-permute-start.9 = (f32[16,64]{1,0:T(8,128)S(1)}, f32[16,64]{1,0:T(8,128)S(1)}, u32[]{:S(2)}, u32[]{:S(2)}) collective-permute-start(f32[16,64]{1,0:T(8,128)S(1)} %bitcast.247), channel_id=1, source_target_pairs={{2,0},{3,1},{4,2},{5,3},{6,4},{7,5},{8,6},{9,7},{10,8},{11,9},{12,... | collective-permute-start | bytes 12296 | tf_op jit(solution)/shard_map/ppermute | solution.py:35
  62.1 8.5 %collective-permute-start.10 = (f32[16,64]{1,0:T(8,128)S(1)}, f32[16,64]{1,0:T(8,128)S(1)}, u32[]{:S(2)}, u32[]{:S(2)}) collective-permute-start(f32[16,64]{1,0:T(8,128)S(1)} %bitcast.248), channel_id=1, source_target_pairs={{3,0},{4,1},{5,2},{6,3},{7,4},{8,5},{9,6},{10,7},{11,8},{12,9},{13... | collective-permute-start | bytes 12296 | tf_op jit(solution)/shard_map/ppermute | solution.py:35
  70.6 3.1 collective-permute-start.11
  73.7 5.4 collective-permute-start.13
  79.0 2.6 collective-permute-start.14
  81.7 4.1 collective-permute-start.15
  85.8 6.5 %collective-permute-start.16 = (f32[16,64]{1,0:T(8,128)S(1)}, f32[16,64]{1,0:T(8,128)S(1)}, u32[]{:S(2)}, u32[]{:S(2)}) collective-permute-start(f32[16,64]{1,0:T(8,128)S(1)} %add.212), channel_id=1, source_target_pairs={{0,2},{1,3},{2,4},{3,5},{4,6},{5,7},{6,8},{7,9},{8,10},{9,11},{10,... | collective-permute-start | bytes 12296 | tf_op jit(solution)/shard_map/ppermute | solution.py:35
  92.3 6.6 %collective-permute-start.21 = (f32[16,64]{1,0:T(8,128)S(1)}, f32[16,64]{1,0:T(8,128)S(1)}, u32[]{:S(2)}, u32[]{:S(2)}) collective-permute-start(f32[16,64]{1,0:T(8,128)S(1)} %fusion.63), channel_id=1, source_target_pairs={{0,2},{1,3},{2,0},{3,1},{4,6},{5,7},{6,4},{7,5},{8,10},{9,11},{10,... | collective-permute-start | bytes 12296 | tf_op jit(solution)/shard_map/ppermute | solution.py:29
  98.9 6.4 %collective-permute-start.17 = (f32[16,64]{1,0:T(8,128)S(1)}, f32[16,64]{1,0:T(8,128)S(1)}, u32[]{:S(2)}, u32[]{:S(2)}) collective-permute-start(f32[16,64]{1,0:T(8,128)S(1)} %add.212), channel_id=1, source_target_pairs={{2,0},{3,1},{4,2},{5,3},{6,4},{7,5},{8,6},{9,7},{10,8},{11,9},{12,... | collective-permute-start | bytes 12296 | tf_op jit(solution)/shard_map/ppermute | solution.py:35
  105.3 3.2 collective-permute-start.18
  108.6 9.9 %collective-permute-start.19 = (f32[16,64]{1,0:T(8,128)S(1)}, f32[16,64]{1,0:T(8,128)S(1)}, u32[]{:S(2)}, u32[]{:S(2)}) collective-permute-start(f32[16,64]{1,0:T(8,128)S(1)} %add.212), channel_id=1, source_target_pairs={{6,0},{7,1},{8,2},{9,3},{10,4},{11,5},{12,6},{13,7},{14,8},{15,9},... | collective-permute-start | bytes 12296 | tf_op jit(solution)/shard_map/ppermute | solution.py:35
  118.5 5.5 collective-permute-start.20
  124.0 4.8 collective-permute-start.22
  128.8 2.6 collective-permute-start.23
  131.4 4.6 collective-permute-start.24
  136.0 3.1 collective-permute-start.25
  139.0 5.8 collective-permute-start.26
  144.8 5.0 collective-permute-start.27
  149.8 1.2 collective-permute-start.28
  150.9 2.8 collective-permute-start.29
  153.7 5.5 collective-permute-start.30
  164.3 426.0 %copy-start.2 = (f32[4,16,1536]{2,1,0:T(8,128)S(1)}, f32[4,16,1536]{2,1,0:T(8,128)}, u32[]{:S(2)}) copy-start(f32[4,16,1536]{2,1,0:T(8,128)} %fusion.98) | copy-start | bytes 1179652
  164.4 426.3 %copy-start.6 = (f32[4,512]{1,0:T(4,128)S(1)}, f32[4,512]{1,0:T(4,128)}, u32[]{:S(2)}) copy-start(f32[4,512]{1,0:T(4,128)} %copy-done.5) | copy-start | bytes 24580
  590.3 1.3 copy-start.1
where the time goes:
time: 598 us; the launch traced here: 592 us
  other arithmetic  285 us (48%)
  starting transfers between devices  79.9 us (13%)
  waiting for transfers between devices  67 us (11%)
  local copies, waits for them, and re-layouts  62.3 us (10%)
  loops' own time  55.4 us (9%)
  matrix products  41 us (7%)
    convert_element_type x24, other arithmetic, dipole_block(): (outer_part - diagonal_part).reshape(3 * leaf_size, 3 * leaf_size)  237 us
    ppermute x24, waiting for transfers between devices, passed_along(): return lax.ppermute(block, axis, route)  62.6 us
    ppermute x24, starting transfers between devices, passed_along(): return lax.ppermute(block, axis, route)  59.9 us
    cond x24, local copies, waits for them, and re-layouts  48 us
    another operation x1, loops' own time, shards(): lax.fori_loop(0, local_leaves, one_leaf, jnp.zeros((local_leaves, vectors...  38.3 us
    dot_general x24, matrix products, live_term(): jnp.dot(rows_here, block.T, preferred_element_type=jnp.float32)  31.6 us
    sub x24, other arithmetic, dipole_block(): between = target_pos[:, :, None] - source_pos[:, None, :]  17.2 us
    another operation x24, loops' own time, one_leaf(): total = lax.cond(source >= 0, live_term, lambda running: running, total)  17.1 us
  transfers between devices with their start and end apart: 31, of which 26 were waited for; matrix products, arithmetic and copies ran while one was open for 2% of the time, Pallas kernels for 0%

commit v1 on v0

v1 whole, which is shorter than its diff:
```python
import functools

import jax
import jax.numpy as jnp
from jax import lax
from jax.experimental import pallas as pl
from jax.experimental.pallas import tpu as pltpu
from jax.sharding import PartitionSpec as P

UP = 3
FEATURES = 128
MESH = pl.DeviceIdType.MESH
F32 = jnp.float32
BF16 = jnp.bfloat16
VMEM = pl.BlockSpec(memory_space=pltpu.VMEM)
SMEM = pl.BlockSpec(memory_space=pltpu.SMEM)


def halves(value):
    high = value.astype(BF16)
    return high, (value - high.astype(F32)).astype(BF16)


def thirds(value):
    high, rest = value.astype(BF16).astype(F32), None
    rest = value - high
    middle = rest.astype(BF16).astype(F32)
    return high, middle, (rest - middle).astype(BF16).astype(F32)


def wide_dot(value, matrix, transposed):
    rows = value.shape[0]
    both = jnp.concatenate(halves(value), axis=0)
    dims = (((1,), (1 if transposed else 0,)), ((), ()))
    out = lax.dot_general(both, matrix, dims, preferred_element_type=F32)
    return out[:rows] + out[rows:]


def exchange(
    n,
    minor,
    probes,
    positions,
    polar,
    basis,
    leaf_transfer,
    cluster_transfer,
    wide,
    sites,
    coefs,
    coef_send,
    coef_recv,
    halo_send,
    halo_recv,
):
    leaves = probes.shape[0]
    me = lax.axis_index("gx") * minor + lax.axis_index("gy")

    def at(device):
        return {"gx": device // minor, "gy": lax.rem(device, minor)}

    barrier = pltpu.get_barrier_semaphore()

    @pl.loop(1, n)
    def _(k):
        pl.semaphore_signal(
            barrier, inc=1, device_id=at(lax.rem(me + k, n)), device_id_type=MESH
        )

    cluster = None
    for t in range(leaves):
        root = jnp.sqrt(polar[pl.ds(t, 1), :])
        coef = None
        for a in range(3):
            scaled = (root * probes[t, a].astype(F32)).astype(BF16)
            wide[leaves + t, a] = scaled
            part = lax.dot_general(
                scaled, basis[t, a], (((1,), (1,)), ((), ())), preferred_element_type=F32
            )
            coef = part if coef is None else coef + part
        carried = wide_dot(coef, leaf_transfer[t], False)
        cluster = carried if cluster is None else cluster + carried
    lifted = wide_dot(cluster, cluster_transfer[0], False)
    coefs[me] = jnp.concatenate([cluster, lifted], axis=1)
    sites[1] = jnp.zeros(sites.shape[1:], F32)
    for a in range(3):
        sites[1, pl.ds(a * leaves, leaves), :] = positions[a]
    pl.semaphore_wait(barrier, n - 1)

    def coef_copy(k, source):
        return pltpu.make_async_remote_copy(
            src_ref=coefs.at[source],
            dst_ref=coefs.at[source],
            send_sem=coef_send.at[k],
            recv_sem=coef_recv.at[source],
            device_id=at(lax.rem(me + k, n)),
            device_id_type=MESH,
        )

    def halo(side, device):
        return (
            pltpu.make_async_remote_copy(
                src_ref=wide.at[pl.ds(leaves, leaves)],
                dst_ref=wide.at[pl.ds(2 * leaves * side, leaves)],
                send_sem=halo_send.at[side, 0],
                recv_sem=halo_recv.at[side, 0],
                device_id=at(device),
                device_id_type=MESH,
            ),
            pltpu.make_async_remote_copy(
                src_ref=sites.at[1],
                dst_ref=sites.at[2 * side],
                send_sem=halo_send.at[side, 1],
                recv_sem=halo_recv.at[side, 1],
                device_id=at(device),
                device_id_type=MESH,
            ),
        )

    after = lax.rem(me + 1, n)
    before = lax.rem(me + n - 1, n)

    @pl.loop(1, n)
    def _(k):
        coef_copy(k, me).start()

    @pl.when(me < n - 1)
    def _():
        for copy in halo(0, after):
            copy.start()

    @pl.when(me > 0)
    def _():
        for copy in halo(1, before):
            copy.start()

    @pl.loop(1, n)
    def _(k):
        coef_copy(k, me).wait_send()
        coef_copy(k, lax.rem(me + k, n)).wait_recv()

    @pl.when(me < n - 1)
    def _():
        for copy in halo(0, after):
            copy.wait_send()
        for copy in halo(1, after):
            copy.wait_recv()

    @pl.when(me > 0)
    def _():
        for copy in halo(1, before):
            copy.wait_send()
        for copy in halo(0, before):
            copy.wait_recv()


def centred(sites, side, leaf, leaves, centre):
    point = [sites[side, pl.ds(a * leaves + leaf, 1), :] for a in range(3)]
    return [point[0] - centre] + point[1:]


def square(point):
    return point[0] * point[0] + point[1] * point[1] + point[2] * point[2]


def apply_operator(
    n,
    minor,
    near_lists,
    cluster_lists,
    upper_lists,
    wide,
    sites,
    coefs,
    polar,
    basis,
    leaf_transfer,
    cluster_transfer,
    upper_transfer,
    cluster_coupling,
    upper_coupling,
    out,
    moments,
    source_rows,
    target_rows,
    rows,
    total,
    level,
):
    leaves = polar.shape[0]
    slots = near_lists.shape[1]
    far_slots = cluster_lists.shape[1]
    vectors = wide.shape[2]
    leaf_size = wide.shape[3]
    rank = basis.shape[2]
    me = lax.axis_index("gx") * minor + lax.axis_index("gy")
    centre = (2 * leaves * me + leaves - 1).astype(F32)
    first = (me - 1) * leaves
    empty = 3 * leaves

    for node in range(n // 2):
        level[node] = coefs[2 * node, :, rank:] + coefs[2 * node + 1, :, rank:]
    for lev in range(1, UP):
        start = n - (n >> lev - 1)
        above = n - (n >> lev)
        for node in range(n >> lev + 1):
            place = start + 2 * node
            level[above + node] = wide_dot(
                level[place], upper_transfer[place], False
            ) + wide_dot(level[place + 1], upper_transfer[place + 1], False)
    fields = []
    for lev in range(UP + 1):
        start = n - (n >> lev - 1) if lev else 0
        place = start + (me >> lev)
        field = None
        for s in range(far_slots):
            if lev == 0:
                source = coefs[cluster_lists[0, s], :, :rank]
                matrix = cluster_coupling[0, s]
            else:
                source = level[start + upper_lists[s, place]]
                matrix = upper_coupling[place, s]
            term = wide_dot(source, matrix, True)
            field = term if field is None else field + term
        fields.append(field)
    down = fields[UP]
    for lev in range(UP - 1, -1, -1):
        if lev == 0:
            matrix = cluster_transfer[0]
        else:
            matrix = upper_transfer[n - (n >> lev - 1) + (me >> lev)]
        down = fields[lev] + wide_dot(down, matrix, True)

    rows[...] = jnp.zeros(rows.shape, F32)
    moments[empty] = jnp.zeros(moments.shape[1:], BF16)

    def fill(point, factor, own):
        base = 0
        for a in range(3):
            one, two, three = thirds(point[a] * factor)
            order = (one, one, two, two, one, three) if own else (one, two, one, two, three, one)
            for k, row in enumerate(order):
                rows[base + k : base + k + 1, :] = row
            base += 6
        norm = thirds(square(point) + (1.0 if own else 0.0))
        ones = jnp.ones_like(norm[0])
        for k in range(3):
            rows[base + k : base + k + 1, :] = norm[k] if own else ones
            rows[base + 3 + k : base + 4 + k, :] = ones if own else norm[k]

    @pl.loop(0, 3 * leaves)
    def _(s):
        point = centred(sites, s // leaves, lax.rem(s, leaves), leaves, centre)
        x = [wide[s, a].astype(F32) for a in range(3)]
        along = point[0] * x[0] + point[1] * x[1] + point[2] * x[2]
        norm = square(point)
        parts = [point[a] * x[b] for a in range(3) for b in range(3)]
        parts += [3.0 * point[a] * along - norm * x[a] for a in range(3)]
        for a in range(3):
            moments[s, a * vectors : (a + 1) * vectors, :] = wide[s, a]
        for k, part in enumerate(parts):
            high, low = halves(part)
            place = (3 + k) * vectors
            moments[s, place : place + vectors, :] = high
            place = (15 + k) * vectors
            moments[s, place : place + vectors, :] = low
        fill(point, -2.0, False)
        source_rows[s] = rows[...].T.astype(BF16)

    @pl.loop(0, leaves)
    def _(t):
        fill(centred(sites, 1, t, leaves, centre), 1.0, True)
        target_rows[t] = rows[...].astype(BF16)

    for t in range(leaves):
        target = target_rows[t]
        for pair in range(0, slots, 2):
            kernels, values = [], []
            for slot in range(pair, min(pair + 2, slots)):
                source = near_lists[t, slot]
                place = jnp.where(source >= 0, source - first, empty)
                site = jnp.where(source >= 0, source - first, leaves + t)
                radius = jnp.dot(source_rows[site], target, preferred_element_type=F32)
                inverse = lax.rsqrt(radius)
                weight = inverse * inverse
                kernels.append((weight * weight * inverse).astype(BF16))
                values.append(moments[place])
            term = jnp.dot(
                jnp.concatenate(values, axis=1),
                jnp.concatenate(kernels, axis=0),
                preferred_element_type=F32,
            )
            if pair == 0:
                total[...] = term
            else:
                total[...] += term

        point = centred(sites, 1, t, leaves, centre)
        norm = square(point) + 1.0
        root = jnp.sqrt(polar[pl.ds(t, 1), :])

        def group(k):
            return total[k * vectors : (k + 1) * vectors, :]

        def both(k):
            return group(3 + k) + group(15 + k)

        plain = [group(a) for a in range(3)]
        cross = [[both(3 * a + b) for b in range(3)] for a in range(3)]
        trace = cross[0][0] + cross[1][1] + cross[2][2]
        inner = point[0] * plain[0] + point[1] * plain[1] + point[2] * plain[2]
        leaf_field = wide_dot(down, leaf_transfer[t], True).astype(BF16)
        for a in range(3):
            value = 3.0 * point[a] * (inner - trace) + both(9 + a) - norm * plain[a]
            for b in range(3):
                value += point[b] * (2.0 * cross[b][a] - 3.0 * cross[a][b])
            far = jnp.dot(leaf_field, basis[t, a], preferred_element_type=F32)
            out[t, a] = ((value + far) * root).astype(BF16)


def shards(
    n,
    minor,
    probes,
    positions,
    polar,
    basis,
    leaf_transfer,
    cluster_transfer,
    upper_transfer,
    cluster_coupling,
    upper_coupling,
    near_lists,
    cluster_lists,
    upper_lists,
):
    leaves, vectors, _, leaf_size = probes.shape
    probes = jnp.transpose(probes, (0, 2, 1, 3))
    basis = jnp.transpose(basis, (0, 2, 1, 3))
    positions = jnp.transpose(positions, (1, 0, 2))
    rank = leaf_transfer.shape[1]
    site_rows = -(-3 * leaves // 8) * 8
    wide, sites, coefs = pl.pallas_call(
        functools.partial(exchange, n, minor),
        out_shape=(
            jax.ShapeDtypeStruct((3 * leaves, 3, vectors, leaf_size), BF16),
            jax.ShapeDtypeStruct((3, site_rows, leaf_size), F32),
            jax.ShapeDtypeStruct((n, vectors, 2 * rank), F32),
        ),
        in_specs=[VMEM] * 6,
        out_specs=(VMEM,) * 3,
        scratch_shapes=[
            pltpu.SemaphoreType.DMA((n,)),
            pltpu.SemaphoreType.DMA((n,)),
            pltpu.SemaphoreType.DMA((2, 2)),
            pltpu.SemaphoreType.DMA((2, 2)),
        ],
        compiler_params=pltpu.CompilerParams(
            collective_id=0, has_side_effects=True, vmem_limit_bytes=24 << 20
        ),
        name="exchange",
    )(probes, positions, polar, basis, leaf_transfer, cluster_transfer)
    groups = 27 * vectors
    applied = pl.pallas_call(
        functools.partial(apply_operator, n, minor),
        out_shape=jax.ShapeDtypeStruct((leaves, 3, vectors, leaf_size), BF16),
        in_specs=[SMEM] * 3 + [VMEM] * 10,
        out_specs=VMEM,
        scratch_shapes=[
            pltpu.VMEM((3 * leaves + 1, groups, leaf_size), BF16),
            pltpu.VMEM((3 * leaves, leaf_size, FEATURES), BF16),
            pltpu.VMEM((leaves, FEATURES, leaf_size), BF16),
            pltpu.VMEM((FEATURES, leaf_size), F32),
            pltpu.VMEM((groups, leaf_size), F32),
            pltpu.VMEM((n, vectors, rank), F32),
        ],
        compiler_params=pltpu.CompilerParams(vmem_limit_bytes=48 << 20),
        name="apply_operator",
    )(
        near_lists,
        cluster_lists,
        upper_lists.T,
        wide,
        sites,
        coefs,
        polar,
        basis,
        leaf_transfer,
        cluster_transfer,
        upper_transfer,
        cluster_coupling,
        upper_coupling,
    )
    return jnp.transpose(applied, (0, 2, 1, 3))


def solution(mesh):
    n = mesh.shape["gx"] * mesh.shape["gy"]
    split = ("groups", "gx", "gy")
    in_specs = (
        P(split, None, None, None),
        P(split, None, None),
        P(split, None),
        P(split, None, None, None),
        P(split, None, None),
        P(split, None, None),
        P("groups", None, None),
        P(split, None, None, None),
        P("groups", None, None, None),
        P(split, None),
        P(split, None),
        P("groups", None),
    )
    return jax.shard_map(
        functools.partial(shards, n, mesh.shape["gy"]),
        mesh=mesh,
        in_specs=in_specs,
        out_specs=P(split, None, None, None),
        check_vma=False,
    )
```

time: 598 us -> 47.9 us (0.08)
  other arithmetic: 285 us -> 0 us
  starting transfers between devices: 79.9 us -> 0 us
  waiting for transfers between devices: 67 us -> 0 us
  loops' own time: 55.4 us -> 0 us
  local copies, waits for them, and re-layouts: 62.3 us -> 12.5 us
  matrix products: 41 us -> 0 us
  Pallas kernels: 0 us -> 34.7 us
    convert_element_type x50 -> x0, other arithmetic: 238 us -> none  [the longest x24 237 us: dipole_block(): (outer_part - diagonal_part).reshape(3 * leaf_size, 3 * leaf_size)]
    ppermute x31 -> x0, starting transfers between devices: 79.9 us -> none  [the longest x24 59.9 us: passed_along(): return lax.ppermute(block, axis, route)]
    ppermute x31 -> x0, waiting for transfers between devices: 67 us -> none  [the longest x24 62.6 us: passed_along(): return lax.ppermute(block, axis, route)]
    another operation x25 -> x0, loops' own time: 55.4 us -> none  [the longest x1 38.3 us: shards(): lax.fori_loop(0, local_leaves, one_leaf, jnp.zeros((local_leaves, vectors...]
    cond x24 -> x0, local copies, waits for them, and re-layouts: 48 us -> none
    dot_general x42 -> x0, matrix products: 41 us -> none  [the longest x24 31.6 us: live_term(): jnp.dot(rows_here, block.T, preferred_element_type=jnp.float32)]
    pallas_call x0 -> x2, Pallas kernels: none -> 34.7 us  [the longest x1 19.9 us: shards(): pl.pallas_call(functools.partial(exchange, n, minor), out_shape=(jax.Shap...]
    mul x48 -> x0, other arithmetic: 21.8 us -> none  [the longest x24 11.3 us: dipole_block(): 3.0 * between[:, :, None, :]]
  transfers between devices with their start and end apart: 31 -> 0, of which waited for: 26 -> 0; matrix products, arithmetic and copies ran while one was open for 2% -> 0% of each run, Pallas kernels for 0% -> 0%
where the time goes in v1:
time: 47.9 us; the launch traced here: 47.2 us
  Pallas kernels  34.7 us (72%)
  local copies, waits for them, and re-layouts  12.5 us (26%)
    pallas_call x1, Pallas kernels, shards(): pl.pallas_call(functools.partial(exchange, n, minor), out_shape=(jax.Shap...  19.9 us
    pallas_call x1, Pallas kernels, shards(): pl.pallas_call(functools.partial(apply_operator, n, minor), out_shape=jax...  14.8 us
    unnamed x32, local copies, waits for them, and re-layouts  12.5 us

profile of v1, /device:TPU:0, one launch (start us, length us, event | category | flops | bytes accessed | tf_op | source)
XLA Modules:
  0.0 47.2 jit_solution(5996437841222381676)
XLA Ops:
  0.0 0.0 copy-start
  0.0 1.1 %copy-done = bf16[4,64,3,512]{3,1,2,0:T(8,128)(2,1)S(1)} copy-done((bf16[4,64,3,512]{3,1,2,0:T(8,128)(2,1)S(1)}, bf16[4,64,3,512]{3,1,2,0:T(8,128)(2,1)}, u32[]{:S(2)}) %copy-start) | copy-done | bytes 786456
  1.1 0.0 copy-start.3
  1.1 0.8 %copy-done.3 = bf16[4,64,64]{2,1,0:T(8,128)(2,1)S(1)} copy-done((bf16[4,64,64]{2,1,0:T(8,128)(2,1)S(1)}, bf16[4,64,64]{2,1,0:T(8,128)(2,1)}, u32[]{:S(2)}) %copy-start.3) | copy-done | bytes 32792
  2.0 0.0 copy-start.5
  2.0 0.9 %copy-done.5 = bf16[4,16,3,512]{3,1,2,0:T(8,128)(2,1)S(1)} copy-done((bf16[4,16,3,512]{3,1,2,0:T(8,128)(2,1)S(1)}, bf16[4,16,3,512]{3,1,2,0:T(8,128)(2,1)}, u32[]{:S(2)}) %copy-start.5) | copy-done | bytes 196632
  2.9 0.0 copy-start.8
  2.9 0.7 %copy-done.8 = bf16[1,64,64]{2,1,0:T(8,128)(2,1)S(1)} copy-done((bf16[1,64,64]{2,1,0:T(8,128)(2,1)S(1)}, bf16[1,64,64]{2,1,0:T(8,128)(2,1)}, u32[]{:S(2)}) %copy-start.8) | copy-done | bytes 8216
  3.6 0.0 copy-start.10
  3.6 0.7 %copy-done.10 = f32[4,512]{1,0:T(4,128)S(1)} copy-done((f32[4,512]{1,0:T(4,128)S(1)}, f32[4,512]{1,0:T(4,128)}, u32[]{:S(2)}) %copy-start.10) | copy-done | bytes 8216
  4.3 0.0 copy-start.12
  4.3 0.7 %copy-done.12 = f32[4,3,512]{2,0,1:T(4,128)S(1)} copy-done((f32[4,3,512]{2,0,1:T(4,128)S(1)}, f32[4,3,512]{2,0,1:T(4,128)}, u32[]{:S(2)}) %copy-start.12) | copy-done | bytes 24600
  5.1 0.0 copy-start.1
  5.1 19.9 %exchange.1 = (bf16[12,3,16,512]{3,2,1,0:T(8,128)(2,1)S(1)}, f32[3,16,512]{2,1,0:T(8,128)S(1)}, f32[16,16,128]{2,1,0:T(8,128)S(1)}) custom-call(bf16[4,3,16,512]{3,2,1,0:T(8,128)(2,1)S(1)} %bitcast.7, f32[3,4,512]{2,1,0:T(4,128)S(1)} %bitcast.8, f32[4,512]{1,0:T(4,128)S(1)} %copy-done.10, bf16[4,3,64,512]{3,2,1,0:T(8,128)(2,1)S(1)} %bitcast.5, ...), custom_call_target="tpu_custom_call" | custom-call | tf_op jit(solution)/shard_map/exchange/pallas_call | solution.py:343
  24.9 0.0 copy-done.1
  24.9 0.0 copy-start.2
  24.9 1.3 %copy-done.2 = bf16[14,6,64,64]{3,2,1,0:T(8,128)(2,1)S(1)} copy-done((bf16[14,6,64,64]{3,2,1,0:T(8,128)(2,1)S(1)}, bf16[14,6,64,64]{3,2,1,0:T(8,128)(2,1)}, u32[]{:S(2)}) %copy-start.2) | copy-done | bytes 688152
  26.3 0.0 copy-start.4
  26.3 0.8 %copy-done.4 = bf16[4,64,64]{2,1,0:T(8,128)(2,1)S(1)} copy-done((bf16[4,64,64]{2,1,0:T(8,128)(2,1)S(1)}, bf16[4,64,64]{2,1,0:T(8,128)(2,1)}, u32[]{:S(2)}) %copy-start.4) | copy-done | bytes 32792
  27.1 0.0 copy-start.6
  27.1 0.9 %copy-done.6 = bf16[12,64,64]{2,1,0:T(8,128)(2,1)S(1)} copy-done((bf16[12,64,64]{2,1,0:T(8,128)(2,1)S(1)}, bf16[12,64,64]{2,1,0:T(8,128)(2,1)}, u32[]{:S(2)}) %copy-start.6) | copy-done | bytes 98328
  28.0 0.0 copy-start.7
  28.0 0.9 %copy-done.7 = bf16[1,6,64,64]{3,2,1,0:T(8,128)(2,1)S(1)} copy-done((bf16[1,6,64,64]{3,2,1,0:T(8,128)(2,1)S(1)}, bf16[1,6,64,64]{3,2,1,0:T(8,128)(2,1)}, u32[]{:S(2)}) %copy-start.7) | copy-done | bytes 49176
  28.9 0.0 copy-start.9
  28.9 0.7 %copy-done.9 = bf16[1,64,64]{2,1,0:T(8,128)(2,1)S(1)} copy-done((bf16[1,64,64]{2,1,0:T(8,128)(2,1)S(1)}, bf16[1,64,64]{2,1,0:T(8,128)(2,1)}, u32[]{:S(2)}) %copy-start.9) | copy-done | bytes 8216
  29.7 0.0 copy-start.11
  29.7 0.7 %copy-done.11 = f32[4,512]{1,0:T(4,128)S(1)} copy-done((f32[4,512]{1,0:T(4,128)S(1)}, f32[4,512]{1,0:T(4,128)}, u32[]{:S(2)}) %copy-start.11) | copy-done | bytes 8216
  30.4 0.0 copy-start.13
  30.4 0.7 %copy-done.13 = s32[14,6]{0,1:T(8,128)S(1)} copy-done((s32[14,6]{0,1:T(8,128)S(1)}, s32[14,6]{0,1:T(8,128)}, u32[]{:S(2)}) %copy-start.13) | copy-done | bytes 360
  31.0 0.0 copy-start.14
  31.0 0.7 %copy-done.14 = s32[4,6]{1,0:T(4,128)S(1)} copy-done((s32[4,6]{1,0:T(4,128)S(1)}, s32[4,6]{1,0:T(4,128)}, u32[]{:S(2)}) %copy-start.14) | copy-done | bytes 120
  31.7 0.0 copy-start.15
  31.7 0.7 %copy-done.15 = s32[1,6]{1,0:T(1,128)S(1)} copy-done((s32[1,6]{1,0:T(1,128)S(1)}, s32[1,6]{1,0:T(1,128)}, u32[]{:S(2)}) %copy-start.15) | copy-done | bytes 48
  32.4 14.8 %apply_operator.1 = bf16[4,3,16,512]{3,2,1,0:T(8,128)(2,1)} custom-call(s32[4,6]{1,0:T(4,128)S(1)} %copy-done.14, s32[1,6]{1,0:T(1,128)S(1)} %copy-done.15, s32[6,14]{1,0:T(8,128)S(1)} %bitcast.9, bf16[12,3,16,512]{3,2,1,0:T(8,128)(2,1)S(1)} %get-tuple-element.8.wide, f32[3,16,512]{2,1,0:T(8,128)S(1)} %get-tuple-element.9.sites, ...), custom_call_target="tpu_custom_call" | custom-call | tf_op jit(solution)/shard_map/apply_operator/pallas_call | solution.py:364
Async XLA Ops:
  0.0 1.1 %copy-start = (bf16[4,64,3,512]{3,1,2,0:T(8,128)(2,1)S(1)}, bf16[4,64,3,512]{3,1,2,0:T(8,128)(2,1)}, u32[]{:S(2)}) copy-start(bf16[4,64,3,512]{3,1,2,0:T(8,128)(2,1)} %param.15) | copy-start | bytes 2359300
  1.1 0.8 %copy-start.3 = (bf16[4,64,64]{2,1,0:T(8,128)(2,1)S(1)}, bf16[4,64,64]{2,1,0:T(8,128)(2,1)}, u32[]{:S(2)}) copy-start(bf16[4,64,64]{2,1,0:T(8,128)(2,1)} %leaf_transfer.3) | copy-start | bytes 98308
  2.0 0.9 %copy-start.5 = (bf16[4,16,3,512]{3,1,2,0:T(8,128)(2,1)S(1)}, bf16[4,16,3,512]{3,1,2,0:T(8,128)(2,1)}, u32[]{:S(2)}) copy-start(bf16[4,16,3,512]{3,1,2,0:T(8,128)(2,1)} %param.12) | copy-start | bytes 589828
  2.9 0.7 %copy-start.8 = (bf16[1,64,64]{2,1,0:T(8,128)(2,1)S(1)}, bf16[1,64,64]{2,1,0:T(8,128)(2,1)}, u32[]{:S(2)}) copy-start(bf16[1,64,64]{2,1,0:T(8,128)(2,1)} %cluster_transfer.3) | copy-start | bytes 24580
  3.6 0.7 %copy-start.10 = (f32[4,512]{1,0:T(4,128)S(1)}, f32[4,512]{1,0:T(4,128)}, u32[]{:S(2)}) copy-start(f32[4,512]{1,0:T(4,128)} %polar.3) | copy-start | bytes 24580
  4.3 0.7 %copy-start.12 = (f32[4,3,512]{2,0,1:T(4,128)S(1)}, f32[4,3,512]{2,0,1:T(4,128)}, u32[]{:S(2)}) copy-start(f32[4,3,512]{2,0,1:T(4,128)} %param.13) | copy-start | bytes 73732
  5.1 19.9 %copy-start.1 = (bf16[4,64,3,512]{3,1,2,0:T(8,128)(2,1)S(1)}, bf16[4,64,3,512]{3,1,2,0:T(8,128)(2,1)}, u32[]{:S(2)}) copy-start(bf16[4,64,3,512]{3,1,2,0:T(8,128)(2,1)} %param.15) | copy-start | bytes 2359300
  24.9 1.3 %copy-start.2 = (bf16[14,6,64,64]{3,2,1,0:T(8,128)(2,1)S(1)}, bf16[14,6,64,64]{3,2,1,0:T(8,128)(2,1)}, u32[]{:S(2)}) copy-start(bf16[14,6,64,64]{3,2,1,0:T(8,128)(2,1)} %upper_coupling.1) | copy-start | bytes 2064388
  26.3 0.8 %copy-start.4 = (bf16[4,64,64]{2,1,0:T(8,128)(2,1)S(1)}, bf16[4,64,64]{2,1,0:T(8,128)(2,1)}, u32[]{:S(2)}) copy-start(bf16[4,64,64]{2,1,0:T(8,128)(2,1)} %leaf_transfer.3) | copy-start | bytes 98308
  27.1 0.9 %copy-start.6 = (bf16[12,64,64]{2,1,0:T(8,128)(2,1)S(1)}, bf16[12,64,64]{2,1,0:T(8,128)(2,1)}, u32[]{:S(2)}) copy-start(bf16[12,64,64]{2,1,0:T(8,128)(2,1)} %upper_transfer.1) | copy-start | bytes 294916
  28.0 0.9 %copy-start.7 = (bf16[1,6,64,64]{3,2,1,0:T(8,128)(2,1)S(1)}, bf16[1,6,64,64]{3,2,1,0:T(8,128)(2,1)}, u32[]{:S(2)}) copy-start(bf16[1,6,64,64]{3,2,1,0:T(8,128)(2,1)} %cluster_coupling.1) | copy-start | bytes 147460
  28.9 0.7 %copy-start.9 = (bf16[1,64,64]{2,1,0:T(8,128)(2,1)S(1)}, bf16[1,64,64]{2,1,0:T(8,128)(2,1)}, u32[]{:S(2)}) copy-start(bf16[1,64,64]{2,1,0:T(8,128)(2,1)} %cluster_transfer.3) | copy-start | bytes 24580
  29.7 0.7 %copy-start.11 = (f32[4,512]{1,0:T(4,128)S(1)}, f32[4,512]{1,0:T(4,128)}, u32[]{:S(2)}) copy-start(f32[4,512]{1,0:T(4,128)} %polar.3) | copy-start | bytes 24580
  30.4 0.7 %copy-start.13 = (s32[14,6]{0,1:T(8,128)S(1)}, s32[14,6]{0,1:T(8,128)}, u32[]{:S(2)}) copy-start(s32[14,6]{0,1:T(8,128)} %param.23) | copy-start | bytes 1012
  31.0 0.7 %copy-start.14 = (s32[4,6]{1,0:T(4,128)S(1)}, s32[4,6]{1,0:T(4,128)}, u32[]{:S(2)}) copy-start(s32[4,6]{1,0:T(4,128)} %near_lists.1) | copy-start | bytes 292
  31.7 0.7 %copy-start.15 = (s32[1,6]{1,0:T(1,128)S(1)}, s32[1,6]{1,0:T(1,128)}, u32[]{:S(2)}) copy-start(s32[1,6]{1,0:T(1,128)} %cluster_lists.1) | copy-start | bytes 76

commit v2 on v1

v2 whole, which is shorter than its diff:
```python
import functools

import jax
import jax.numpy as jnp
from jax import lax
from jax.experimental import pallas as pl
from jax.experimental.pallas import tpu as pltpu
from jax.sharding import PartitionSpec as P

UP = 3
FEATURES = 128
GROUP = 2
MESH = pl.DeviceIdType.MESH
F32 = jnp.float32
BF16 = jnp.bfloat16
SMEM = pl.BlockSpec(memory_space=pltpu.SMEM)
ANY = pl.BlockSpec(memory_space=pl.ANY)


def halves(value):
    high = value.astype(BF16)
    return high, (value - high.astype(F32)).astype(BF16)


def thirds(value):
    high, rest = value.astype(BF16).astype(F32), None
    rest = value - high
    middle = rest.astype(BF16).astype(F32)
    return high, middle, (rest - middle).astype(BF16).astype(F32)


def wide_dot(value, matrix, transposed):
    rows = value.shape[0]
    both = jnp.concatenate(halves(value), axis=0)
    dims = (((1,), (1 if transposed else 0,)), ((), ()))
    out = lax.dot_general(both, matrix, dims, preferred_element_type=F32)
    return out[:rows] + out[rows:]


def centred(sites, side, leaf, leaves, centre):
    point = [sites[side, pl.ds(a * leaves + leaf, 1), :] for a in range(3)]
    return [point[0] - centre] + point[1:]


def square(point):
    return point[0] * point[0] + point[1] * point[1] + point[2] * point[2]


def apply_operator(
    n,
    minor,
    probes_hbm,
    positions_hbm,
    polar_hbm,
    basis_hbm,
    leaf_transfer_hbm,
    cluster_transfer_hbm,
    upper_transfer_hbm,
    cluster_coupling_hbm,
    upper_coupling_hbm,
    near_lists,
    cluster_lists,
    upper_lists,
    out,
    probes,
    positions,
    polar,
    basis,
    leaf_transfer,
    cluster_transfer,
    upper_transfer,
    coupling,
    wide,
    sites,
    coefs,
    moments,
    source_rows,
    target_rows,
    rows,
    total,
    level,
    load_sem,
    coupling_sem,
    coef_send,
    coef_recv,
    halo_send,
    halo_recv,
):
    leaves = probes.shape[0]
    slots = near_lists.shape[1]
    far_slots = cluster_lists.shape[1]
    vectors = wide.shape[2]
    rank = basis.shape[2]
    me = lax.axis_index("gx") * minor + lax.axis_index("gy")

    def at(device):
        return {"gx": device // minor, "gy": lax.rem(device, minor)}

    def place_of(lev):
        return n - (n >> lev - 1) + (me >> lev)

    def load(k, source, target):
        copy = pltpu.make_async_copy(source, target, load_sem.at[k])
        copy.start()
        return copy

    barrier = pltpu.get_barrier_semaphore()

    @pl.loop(1, n)
    def _(k):
        pl.semaphore_signal(
            barrier, inc=1, device_id=at(lax.rem(me + k, n)), device_id_type=MESH
        )

    first_loads = [
        load(0, polar_hbm, polar),
        load(1, probes_hbm, probes),
        load(2, positions_hbm, positions),
    ]
    basis_loads = [
        load(3, basis_hbm, basis),
        load(4, leaf_transfer_hbm, leaf_transfer),
        load(5, cluster_transfer_hbm, cluster_transfer),
    ]
    far_loads = [
        load(6, upper_transfer_hbm, upper_transfer),
        load(7, cluster_coupling_hbm.at[0], coupling.at[0]),
    ]
    for lev in range(1, UP + 1):
        copy = pltpu.make_async_copy(
            upper_coupling_hbm.at[place_of(lev)], coupling.at[lev], coupling_sem.at[lev]
        )
        copy.start()
        far_loads.append(copy)

    def coef_copy(k, source):
        return pltpu.make_async_remote_copy(
            src_ref=coefs.at[source],
            dst_ref=coefs.at[source],
            send_sem=coef_send.at[k],
            recv_sem=coef_recv.at[source],
            device_id=at(lax.rem(me + k, n)),
            device_id_type=MESH,
        )

    def halo(side, device):
        return (
            pltpu.make_async_remote_copy(
                src_ref=sites.at[1],
                dst_ref=sites.at[2 * side],
                send_sem=halo_send.at[side, 1],
                recv_sem=halo_recv.at[side, 1],
                device_id=at(device),
                device_id_type=MESH,
            ),
            pltpu.make_async_remote_copy(
                src_ref=wide.at[pl.ds(leaves, leaves)],
                dst_ref=wide.at[pl.ds(2 * leaves * side, leaves)],
                send_sem=halo_send.at[side, 0],
                recv_sem=halo_recv.at[side, 0],
                device_id=at(device),
                device_id_type=MESH,
            ),
        )

    after = lax.rem(me + 1, n)
    before = lax.rem(me + n - 1, n)

    for copy in first_loads:
        copy.wait()
    for t in range(leaves):
        root = jnp.sqrt(polar[pl.ds(t, 1), :])
        for a in range(3):
            wide[leaves + t, a] = (root * probes[t, a].astype(F32)).astype(BF16)
    sites[1] = jnp.zeros(sites.shape[1:], F32)
    for a in range(3):
        sites[1, pl.ds(a * leaves, leaves), :] = positions[a]
    pl.semaphore_wait(barrier, n - 1)

    @pl.when(me < n - 1)
    def _():
        for copy in halo(0, after):
            copy.start()

    @pl.when(me > 0)
    def _():
        for copy in halo(1, before):
            copy.start()

    for copy in basis_loads:
        copy.wait()
    cluster = None
    for t in range(leaves):
        coef = None
        for a in range(3):
            part = lax.dot_general(
                wide[leaves + t, a], basis[t, a], (((1,), (1,)), ((), ())), preferred_element_type=F32
            )
            coef = part if coef is None else coef + part
        carried = wide_dot(coef, leaf_transfer[t], False)
        cluster = carried if cluster is None else cluster + carried
    lifted = wide_dot(cluster, cluster_transfer[0], False)
    coefs[me] = jnp.concatenate([cluster, lifted], axis=1)

    @pl.loop(1, n)
    def _(k):
        coef_copy(k, me).start()

    centre = (2 * leaves * me + leaves - 1).astype(F32)
    first = (me - 1) * leaves
    empty = 3 * leaves
    rows[...] = jnp.zeros(rows.shape, F32)
    moments[empty] = jnp.zeros(moments.shape[1:], BF16)

    def fill(point, factor, own):
        base = 0
        for a in range(3):
            one, two, three = thirds(point[a] * factor)
            order = (one, one, two, two, one, three) if own else (one, two, one, two, three, one)
            for k, row in enumerate(order):
                rows[base + k : base + k + 1, :] = row
            base += 6
        norm = thirds(square(point) + (1.0 if own else 0.0))
        ones = jnp.ones_like(norm[0])
        for k in range(3):
            rows[base + k : base + k + 1, :] = norm[k] if own else ones
            rows[base + 3 + k : base + 4 + k, :] = ones if own else norm[k]

    def prepare(side, leaf):
        s = side * leaves + leaf
        point = centred(sites, side, leaf, leaves, centre)
        x = [wide[s, a].astype(F32) for a in range(3)]
        along = point[0] * x[0] + point[1] * x[1] + point[2] * x[2]
        norm = square(point)
        parts = [point[a] * x[b] for a in range(3) for b in range(3)]
        parts += [3.0 * point[a] * along - norm * x[a] for a in range(3)]
        for a in range(3):
            moments[s, a * vectors : (a + 1) * vectors, :] = wide[s, a]
        for k, part in enumerate(parts):
            high, low = halves(part)
            place = (3 + k) * vectors
            moments[s, place : place + vectors, :] = high
            place = (15 + k) * vectors
            moments[s, place : place + vectors, :] = low
        fill(point, -2.0, False)
        source_rows[s] = rows[...].T.astype(BF16)

    def kernel_matrix(site, target):
        radius = jnp.dot(source_rows[site], target, preferred_element_type=F32)
        inverse = lax.rsqrt(radius)
        weight = inverse * inverse
        return (weight * weight * inverse).astype(BF16)

    @pl.loop(0, leaves)
    def _(t):
        prepare(1, t)
        fill(centred(sites, 1, t, leaves, centre), 1.0, True)
        target_rows[t] = rows[...].astype(BF16)

    @pl.loop(0, leaves)
    def _(t):
        matrix = kernel_matrix(leaves + t, target_rows[t])
        total[t] = jnp.dot(moments[leaves + t], matrix, preferred_element_type=F32)

    for copy in far_loads:
        copy.wait()

    @pl.loop(1, n)
    def _(k):
        coef_copy(k, lax.rem(me + k, n)).wait_recv()

    for node in range(n // 2):
        level[node] = coefs[2 * node, :, rank:] + coefs[2 * node + 1, :, rank:]
    for lev in range(1, UP):
        start = n - (n >> lev - 1)
        above = n - (n >> lev)
        for node in range(n >> lev + 1):
            place = start + 2 * node
            level[above + node] = wide_dot(
                level[place], upper_transfer[place], False
            ) + wide_dot(level[place + 1], upper_transfer[place + 1], False)
    fields = []
    for lev in range(UP + 1):
        field = None
        for s in range(far_slots):
            if lev == 0:
                source = coefs[cluster_lists[0, s], :, :rank]
            else:
                source = level[n - (n >> lev - 1) + upper_lists[s, place_of(lev)]]
            term = wide_dot(source, coupling[lev, s], True)
            field = term if field is None else field + term
        fields.append(field)
    down = fields[UP]
    for lev in range(UP - 1, -1, -1):
        matrix = upper_transfer[place_of(lev)] if lev else cluster_transfer[0]
        down = fields[lev] + wide_dot(down, matrix, True)

    @pl.when(me > 0)
    def _():
        for copy in halo(0, before):
            copy.wait_recv()

    @pl.when(me < n - 1)
    def _():
        for copy in halo(1, after):
            copy.wait_recv()

    @pl.loop(0, leaves)
    def _(t):
        prepare(0, t)

    @pl.loop(0, leaves)
    def _(t):
        prepare(2, t)

    for t in range(leaves):
        target = target_rows[t]
        for begin in range(1, slots, GROUP):
            kernels, values = [], []
            for slot in range(begin, min(begin + GROUP, slots)):
                source = near_lists[t, slot]
                site = jnp.clip(source - first, 0, empty - 1)
                place = jnp.where(source >= 0, site, empty)
                kernels.append(kernel_matrix(jnp.where(source >= 0, site, leaves + t), target))
                values.append(moments[place])
            total[t] += jnp.dot(
                jnp.concatenate(values, axis=1),
                jnp.concatenate(kernels, axis=0),
                preferred_element_type=F32,
            )

        point = centred(sites, 1, t, leaves, centre)
        norm = square(point) + 1.0
        root = jnp.sqrt(polar[pl.ds(t, 1), :])

        def group(k):
            return total[t, k * vectors : (k + 1) * vectors, :]

        def both(k):
            return group(3 + k) + group(15 + k)

        plain = [group(a) for a in range(3)]
        cross = [[both(3 * a + b) for b in range(3)] for a in range(3)]
        trace = cross[0][0] + cross[1][1] + cross[2][2]
        inner = point[0] * plain[0] + point[1] * plain[1] + point[2] * plain[2]
        leaf_field = wide_dot(down, leaf_transfer[t], True).astype(BF16)
        for a in range(3):
            value = 3.0 * point[a] * (inner - trace) + both(9 + a) - norm * plain[a]
            for b in range(3):
                value += point[b] * (2.0 * cross[b][a] - 3.0 * cross[a][b])
            far = jnp.dot(leaf_field, basis[t, a], preferred_element_type=F32)
            out[t, a] = ((value + far) * root).astype(BF16)

    @pl.loop(1, n)
    def _(k):
        coef_copy(k, me).wait_send()

    @pl.when(me < n - 1)
    def _():
        for copy in halo(0, after):
            copy.wait_send()

    @pl.when(me > 0)
    def _():
        for copy in halo(1, before):
            copy.wait_send()


def shards(
    n,
    minor,
    probes,
    positions,
    polar,
    basis,
    leaf_transfer,
    cluster_transfer,
    upper_transfer,
    cluster_coupling,
    upper_coupling,
    near_lists,
    cluster_lists,
    upper_lists,
):
    leaves, vectors, _, leaf_size = probes.shape
    probes = jnp.transpose(probes, (0, 2, 1, 3))
    basis = jnp.transpose(basis, (0, 2, 1, 3))
    positions = jnp.transpose(positions, (1, 0, 2))
    rank = leaf_transfer.shape[1]
    site_rows = -(-3 * leaves // 8) * 8
    groups = 27 * vectors
    slots = cluster_coupling.shape[1]

    def like(array):
        return pltpu.VMEM(array.shape, array.dtype)

    applied = pl.pallas_call(
        functools.partial(apply_operator, n, minor),
        out_shape=jax.ShapeDtypeStruct((leaves, 3, vectors, leaf_size), BF16),
        in_specs=[ANY] * 9 + [SMEM] * 3,
        out_specs=pl.BlockSpec(memory_space=pltpu.VMEM),
        scratch_shapes=[
            like(probes),
            like(positions),
            like(polar),
            like(basis),
            like(leaf_transfer),
            like(cluster_transfer),
            like(upper_transfer),
            pltpu.VMEM((UP + 1, slots, rank, rank), BF16),
            pltpu.VMEM((3 * leaves, 3, vectors, leaf_size), BF16),
            pltpu.VMEM((3, site_rows, leaf_size), F32),
            pltpu.VMEM((n, vectors, 2 * rank), F32),
            pltpu.VMEM((3 * leaves + 1, groups, leaf_size), BF16),
            pltpu.VMEM((3 * leaves, leaf_size, FEATURES), BF16),
            pltpu.VMEM((leaves, FEATURES, leaf_size), BF16),
            pltpu.VMEM((FEATURES, leaf_size), F32),
            pltpu.VMEM((leaves, groups, leaf_size), F32),
            pltpu.VMEM((n, vectors, rank), F32),
            pltpu.SemaphoreType.DMA((8,)),
            pltpu.SemaphoreType.DMA((UP + 1,)),
            pltpu.SemaphoreType.DMA((n,)),
            pltpu.SemaphoreType.DMA((n,)),
            pltpu.SemaphoreType.DMA((2, 2)),
            pltpu.SemaphoreType.DMA((2, 2)),
        ],
        compiler_params=pltpu.CompilerParams(
            collective_id=0, has_side_effects=True, vmem_limit_bytes=56 << 20
        ),
        name="apply_operator",
    )(
        probes,
        positions,
        polar,
        basis,
        leaf_transfer,
        cluster_transfer,
        upper_transfer,
        cluster_coupling,
        upper_coupling,
        near_lists,
        cluster_lists,
        upper_lists.T,
    )
    return jnp.transpose(applied, (0, 2, 1, 3))


def solution(mesh):
    n = mesh.shape["gx"] * mesh.shape["gy"]
    split = ("groups", "gx", "gy")
    in_specs = (
        P(split, None, None, None),
        P(split, None, None),
        P(split, None),
        P(split, None, None, None),
        P(split, None, None),
        P(split, None, None),
        P("groups", None, None),
        P(split, None, None, None),
        P("groups", None, None, None),
        P(split, None),
        P(split, None),
        P("groups", None),
    )
    return jax.shard_map(
        functools.partial(shards, n, mesh.shape["gy"]),
        mesh=mesh,
        in_specs=in_specs,
        out_specs=P(split, None, None, None),
        check_vma=False,
    )
```

time: 47.9 us -> 35.5 us (0.74)
  local copies, waits for them, and re-layouts: 12.5 us -> 1.62 us
  Pallas kernels: 34.7 us -> 33.7 us
    pallas_call x1 -> x0, Pallas kernels: 19.9 us -> none  [shards(): pl.pallas_call(functools.partial(exchange, n, minor), out_shape=(jax.Shap...]
    pallas_call x1, Pallas kernels: 14.8 us -> 33.7 us  [shards(): pl.pallas_call(functools.partial(apply_operator, n, minor), out_shape=jax...]
    unnamed x32 -> x1, local copies, waits for them, and re-layouts: 12.5 us -> 1.62 us
where the time goes in v2:
time: 35.5 us; the launch traced here: 35.3 us
  Pallas kernels  33.7 us (95%)
  local copies, waits for them, and re-layouts  1.62 us (5%)
    pallas_call x1, Pallas kernels, shards(): pl.pallas_call(functools.partial(apply_operator, n, minor), out_shape=jax...  33.7 us
    unnamed x1, local copies, waits for them, and re-layouts  1.62 us

profile of v2, /device:TPU:0, one launch (start us, length us, event | category | flops | bytes accessed | tf_op | source)
XLA Modules:
  0.0 35.3 jit_solution(10038514069657332369)
XLA Ops:
  0.0 33.7 %apply_operator.1 = bf16[4,3,16,512]{3,2,1,0:T(8,128)(2,1)} custom-call(bf16[4,3,16,512]{3,2,1,0:T(8,128)(2,1)} %bitcast.7, f32[3,4,512]{2,1,0:T(4,128)} %bitcast.8, f32[4,512]{1,0:T(4,128)} %polar_hbm.1, bf16[4,3,64,512]{3,2,1,0:T(8,128)(2,1)} %bitcast.6, bf16[4,64,64]{2,1,0:T(8,128)(2,1)} %leaf_transfer_hbm.1, bf16[1,64,64]{2,1,0:T(8,128)(2,1)} %cluster_transfer_hbm.1, ...), custom_call_target="tpu_custom_call" | custom-call | tf_op jit(solution)/shard_map/apply_operator/pallas_call | solution.py:397
  33.7 1.6 %copy.14 = bf16[4,16,3,512]{3,1,2,0:T(8,128)(2,1)} copy(bf16[4,16,3,512]{3,1,2,0:T(8,128)(2,1)} %bitcast.5) | data formatting | bytes 393216

commit v3 on v2

--- a/solution.py
+++ b/solution.py
@@ -9,11 +9,9 @@
 
 UP = 3
 FEATURES = 128
-GROUP = 2
 MESH = pl.DeviceIdType.MESH
 F32 = jnp.float32
 BF16 = jnp.bfloat16
-SMEM = pl.BlockSpec(memory_space=pltpu.SMEM)
 ANY = pl.BlockSpec(memory_space=pl.ANY)
 
 
@@ -58,9 +56,9 @@
     upper_transfer_hbm,
     cluster_coupling_hbm,
     upper_coupling_hbm,
-    near_lists,
-    cluster_lists,
-    upper_lists,
+    near_lists_hbm,
+    cluster_lists_hbm,
+    upper_lists_hbm,
     out,
     probes,
     positions,
@@ -78,7 +76,11 @@
     target_rows,
     rows,
     total,
+    matrices,
     level,
+    near_lists,
+    cluster_lists,
+    upper_lists,
     load_sem,
     coupling_sem,
     coef_send,
@@ -90,6 +92,7 @@
     slots = near_lists.shape[1]
     far_slots = cluster_lists.shape[1]
     vectors = wide.shape[2]
+    leaf_size = wide.shape[3]
     rank = basis.shape[2]
     me = lax.axis_index("gx") * minor + lax.axis_index("gy")
 
@@ -113,14 +116,19 @@
         )
 
     first_loads = [
+        load(2, positions_hbm, positions),
         load(0, polar_hbm, polar),
         load(1, probes_hbm, probes),
-        load(2, positions_hbm, positions),
     ]
     basis_loads = [
         load(3, basis_hbm, basis),
         load(4, leaf_transfer_hbm, leaf_transfer),
         load(5, cluster_transfer_hbm, cluster_transfer),
+    ]
+    list_loads = [
+        load(8, near_lists_hbm, near_lists),
+        load(9, cluster_lists_hbm, cluster_lists),
+        load(10, upper_lists_hbm, upper_lists),
     ]
     far_loads = [
         load(6, upper_transfer_hbm, upper_transfer),
@@ -166,15 +174,16 @@
     after = lax.rem(me + 1, n)
     before = lax.rem(me + n - 1, n)
 
-    for copy in first_loads:
+    first_loads[0].wait()
+    sites[1] = jnp.zeros(sites.shape[1:], F32)
+    for a in range(3):
+        sites[1, pl.ds(a * leaves, leaves), :] = positions[a]
+    for copy in first_loads[1:]:
         copy.wait()
     for t in range(leaves):
         root = jnp.sqrt(polar[pl.ds(t, 1), :])
         for a in range(3):
             wide[leaves + t, a] = (root * probes[t, a].astype(F32)).astype(BF16)
-    sites[1] = jnp.zeros(sites.shape[1:], F32)
-    for a in range(3):
-        sites[1, pl.ds(a * leaves, leaves), :] = positions[a]
     pl.semaphore_wait(barrier, n - 1)
 
     @pl.when(me < n - 1)
@@ -242,8 +251,10 @@
             moments[s, place : place + vectors, :] = high
             place = (15 + k) * vectors
             moments[s, place : place + vectors, :] = low
-        fill(point, -2.0, False)
-        source_rows[s] = rows[...].T.astype(BF16)
+
+    def prepare_rows(side, leaf):
+        fill(centred(sites, side, leaf, leaves, centre), -2.0, False)
+        source_rows[side * leaves + leaf] = rows[...].T.astype(BF16)
 
     def kernel_matrix(site, target):
         radius = jnp.dot(source_rows[site], target, preferred_element_type=F32)
@@ -254,6 +265,7 @@
     @pl.loop(0, leaves)
     def _(t):
         prepare(1, t)
+        prepare_rows(1, t)
         fill(centred(sites, 1, t, leaves, centre), 1.0, True)
         target_rows[t] = rows[...].astype(BF16)
 
@@ -261,6 +273,34 @@
     def _(t):
         matrix = kernel_matrix(leaves + t, target_rows[t])
         total[t] = jnp.dot(moments[leaves + t], matrix, preferred_element_type=F32)
+
+    @pl.when(me > 0)
+    def _():
+        halo(0, before)[0].wait_recv()
+
+    @pl.when(me < n - 1)
+    def _():
+        halo(1, after)[0].wait_recv()
+
+    for copy in list_loads:
+        copy.wait()
+
+    @pl.loop(0, leaves)
+    def _(t):
+        prepare_rows(0, t)
+        prepare_rows(2, t)
+
+    def site_of(t, slot):
+        source = near_lists[t, slot]
+        return source, jnp.clip(source - first, 0, empty - 1)
+
+    @pl.loop(0, leaves)
+    def _(t):
+        target = target_rows[t]
+        for slot in range(1, slots):
+            source, site = site_of(t, slot)
+            block = kernel_matrix(jnp.where(source >= 0, site, leaves + t), target)
+            matrices[t, (slot - 1) * leaf_size : slot * leaf_size, :] = block
 
     for copy in far_loads:
         copy.wait()
@@ -297,37 +337,25 @@
 
     @pl.when(me > 0)
     def _():
-        for copy in halo(0, before):
-            copy.wait_recv()
+        halo(0, before)[1].wait_recv()
 
     @pl.when(me < n - 1)
     def _():
-        for copy in halo(1, after):
-            copy.wait_recv()
+        halo(1, after)[1].wait_recv()
 
     @pl.loop(0, leaves)
     def _(t):
         prepare(0, t)
-
-    @pl.loop(0, leaves)
-    def _(t):
         prepare(2, t)
 
     for t in range(leaves):
-        target = target_rows[t]
-        for begin in range(1, slots, GROUP):
-            kernels, values = [], []
-            for slot in range(begin, min(begin + GROUP, slots)):
-                source = near_lists[t, slot]
-                site = jnp.clip(source - first, 0, empty - 1)
-                place = jnp.where(source >= 0, site, empty)
-                kernels.append(kernel_matrix(jnp.where(source >= 0, site, leaves + t), target))
-                values.append(moments[place])
-            total[t] += jnp.dot(
-                jnp.concatenate(values, axis=1),
-                jnp.concatenate(kernels, axis=0),
-                preferred_element_type=F32,
-            )
+        values = []
+        for slot in range(1, slots):
+            source, site = site_of(t, slot)
+            values.append(moments[jnp.where(source >= 0, site, empty)])
+        total[t] += jnp.dot(
+            jnp.concatenate(values, axis=1), matrices[t], preferred_element_type=F32
+        )
 
         point = centred(sites, 1, t, leaves, centre)
         norm = square(point) + 1.0
@@ -397,7 +425,7 @@
     applied = pl.pallas_call(
         functools.partial(apply_operator, n, minor),
         out_shape=jax.ShapeDtypeStruct((leaves, 3, vectors, leaf_size), BF16),
-        in_specs=[ANY] * 9 + [SMEM] * 3,
+        in_specs=[ANY] * 12,
         out_specs=pl.BlockSpec(memory_space=pltpu.VMEM),
         scratch_shapes=[
             like(probes),
@@ -416,8 +444,12 @@
             pltpu.VMEM((leaves, FEATURES, leaf_size), BF16),
             pltpu.VMEM((FEATURES, leaf_size), F32),
             pltpu.VMEM((leaves, groups, leaf_size), F32),
+            pltpu.VMEM((leaves, (near_lists.shape[1] - 1) * leaf_size, leaf_size), BF16),
             pltpu.VMEM((n, vectors, rank), F32),
-            pltpu.SemaphoreType.DMA((8,)),
+            pltpu.SMEM(near_lists.shape, jnp.int32),
+            pltpu.SMEM(cluster_lists.shape, jnp.int32),
+            pltpu.SMEM(upper_lists.shape[::-1], jnp.int32),
+            pltpu.SemaphoreType.DMA((11,)),
             pltpu.SemaphoreType.DMA((UP + 1,)),
             pltpu.SemaphoreType.DMA((n,)),
             pltpu.SemaphoreType.DMA((n,)),

time: 35.5 us -> 30.3 us (0.85)
  Pallas kernels: 33.7 us -> 28.5 us
    pallas_call x1, Pallas kernels: 33.7 us -> 28.5 us  [shards(): pl.pallas_call(functools.partial(apply_operator, n, minor), out_shape=jax...]
where the time goes in v3:
time: 30.3 us; the launch traced here: 30.2 us
  Pallas kernels  28.5 us (94%)
  local copies, waits for them, and re-layouts  1.62 us (5%)
    pallas_call x1, Pallas kernels, shards(): pl.pallas_call(functools.partial(apply_operator, n, minor), out_shape=jax...  28.5 us
    unnamed x1, local copies, waits for them, and re-layouts  1.62 us

profile of v3, /device:TPU:0, one launch (start us, length us, event | category | flops | bytes accessed | tf_op | source)
XLA Modules:
  0.0 30.2 jit_solution(7615958422576053687)
XLA Ops:
  0.0 28.5 %apply_operator.1 = bf16[4,3,16,512]{3,2,1,0:T(8,128)(2,1)} custom-call(bf16[4,3,16,512]{3,2,1,0:T(8,128)(2,1)} %bitcast.7, f32[3,4,512]{2,1,0:T(4,128)} %bitcast.8, f32[4,512]{1,0:T(4,128)} %polar_hbm.1, bf16[4,3,64,512]{3,2,1,0:T(8,128)(2,1)} %bitcast.6, bf16[4,64,64]{2,1,0:T(8,128)(2,1)} %leaf_transfer_hbm.1, bf16[1,64,64]{2,1,0:T(8,128)(2,1)} %cluster_transfer_hbm.1, ...), custom_call_target="tpu_custom_call" | custom-call | tf_op jit(solution)/shard_map/apply_operator/pallas_call | solution.py:425
  28.5 1.6 %copy.14 = bf16[4,16,3,512]{3,1,2,0:T(8,128)(2,1)} copy(bf16[4,16,3,512]{3,1,2,0:T(8,128)(2,1)} %bitcast.5) | data formatting | bytes 393216

commit v4 on v3

--- a/solution.py
+++ b/solution.py
@@ -9,6 +9,7 @@
 
 UP = 3
 FEATURES = 128
+USED = 32
 MESH = pl.DeviceIdType.MESH
 F32 = jnp.float32
 BF16 = jnp.bfloat16
@@ -35,8 +36,8 @@
     return out[:rows] + out[rows:]
 
 
-def centred(sites, side, leaf, leaves, centre):
-    point = [sites[side, pl.ds(a * leaves + leaf, 1), :] for a in range(3)]
+def centred(positions, side, leaf, centre):
+    point = [positions[side, a, pl.ds(leaf, 1), :] for a in range(3)]
     return [point[0] - centre] + point[1:]
 
 
@@ -69,7 +70,6 @@
     upper_transfer,
     coupling,
     wide,
-    sites,
     coefs,
     moments,
     source_rows,
@@ -88,7 +88,7 @@
     halo_send,
     halo_recv,
 ):
-    leaves = probes.shape[0]
+    leaves = probes.shape[1]
     slots = near_lists.shape[1]
     far_slots = cluster_lists.shape[1]
     vectors = wide.shape[2]
@@ -116,9 +116,9 @@
         )
 
     first_loads = [
-        load(2, positions_hbm, positions),
-        load(0, polar_hbm, polar),
-        load(1, probes_hbm, probes),
+        load(2, positions_hbm, positions.at[1]),
+        load(0, polar_hbm, polar.at[1]),
+        load(1, probes_hbm, probes.at[1]),
     ]
     basis_loads = [
         load(3, basis_hbm, basis),
@@ -151,50 +151,49 @@
             device_id_type=MESH,
         )
 
-    def halo(side, device):
-        return (
-            pltpu.make_async_remote_copy(
-                src_ref=sites.at[1],
-                dst_ref=sites.at[2 * side],
-                send_sem=halo_send.at[side, 1],
-                recv_sem=halo_recv.at[side, 1],
-                device_id=at(device),
-                device_id_type=MESH,
-            ),
-            pltpu.make_async_remote_copy(
-                src_ref=wide.at[pl.ds(leaves, leaves)],
-                dst_ref=wide.at[pl.ds(2 * leaves * side, leaves)],
-                send_sem=halo_send.at[side, 0],
-                recv_sem=halo_recv.at[side, 0],
-                device_id=at(device),
-                device_id_type=MESH,
-            ),
+    def halo(side, part, device):
+        source, target = (
+            (positions_hbm, positions),
+            (polar_hbm, polar),
+            (probes_hbm, probes),
+        )[part]
+        return pltpu.make_async_remote_copy(
+            src_ref=source,
+            dst_ref=target.at[2 * side],
+            send_sem=halo_send.at[side, part],
+            recv_sem=halo_recv.at[side, part],
+            device_id=at(device),
+            device_id_type=MESH,
         )
 
     after = lax.rem(me + 1, n)
     before = lax.rem(me + n - 1, n)
 
-    first_loads[0].wait()
-    sites[1] = jnp.zeros(sites.shape[1:], F32)
-    for a in range(3):
-        sites[1, pl.ds(a * leaves, leaves), :] = positions[a]
-    for copy in first_loads[1:]:
+    rows[...] = jnp.zeros(rows.shape, F32)
+    source_rows[...] = jnp.zeros(source_rows.shape, BF16)
+    moments[3 * leaves] = jnp.zeros(moments.shape[1:], BF16)
+    pl.semaphore_wait(barrier, n - 1)
+
+    @pl.when(me < n - 1)
+    def _():
+        for part in range(3):
+            halo(0, part, after).start()
+
+    @pl.when(me > 0)
+    def _():
+        for part in range(3):
+            halo(1, part, before).start()
+
+    for copy in first_loads:
         copy.wait()
+
+    def scaled_probes(side, leaf):
+        root = jnp.sqrt(polar[side, pl.ds(leaf, 1), :])
+        return [(root * probes[side, leaf, a].astype(F32)).astype(BF16) for a in range(3)]
+
     for t in range(leaves):
-        root = jnp.sqrt(polar[pl.ds(t, 1), :])
-        for a in range(3):
-            wide[leaves + t, a] = (root * probes[t, a].astype(F32)).astype(BF16)
-    pl.semaphore_wait(barrier, n - 1)
-
-    @pl.when(me < n - 1)
-    def _():
-        for copy in halo(0, after):
-            copy.start()
-
-    @pl.when(me > 0)
-    def _():
-        for copy in halo(1, before):
-            copy.start()
+        for a, value in enumerate(scaled_probes(1, t)):
+            wide[t, a] = value
 
     for copy in basis_loads:
         copy.wait()
@@ -203,7 +202,7 @@
         coef = None
         for a in range(3):
             part = lax.dot_general(
-                wide[leaves + t, a], basis[t, a], (((1,), (1,)), ((), ())), preferred_element_type=F32
+                wide[t, a], basis[t, a], (((1,), (1,)), ((), ())), preferred_element_type=F32
             )
             coef = part if coef is None else coef + part
         carried = wide_dot(coef, leaf_transfer[t], False)
@@ -218,8 +217,6 @@
     centre = (2 * leaves * me + leaves - 1).astype(F32)
     first = (me - 1) * leaves
     empty = 3 * leaves
-    rows[...] = jnp.zeros(rows.shape, F32)
-    moments[empty] = jnp.zeros(moments.shape[1:], BF16)
 
     def fill(point, factor, own):
         base = 0
@@ -237,14 +234,15 @@
 
     def prepare(side, leaf):
         s = side * leaves + leaf
-        point = centred(sites, side, leaf, leaves, centre)
-        x = [wide[s, a].astype(F32) for a in range(3)]
+        point = centred(positions, side, leaf, centre)
+        held = scaled_probes(side, leaf) if side != 1 else [wide[leaf, a] for a in range(3)]
+        x = [held[a].astype(F32) for a in range(3)]
         along = point[0] * x[0] + point[1] * x[1] + point[2] * x[2]
         norm = square(point)
         parts = [point[a] * x[b] for a in range(3) for b in range(3)]
         parts += [3.0 * point[a] * along - norm * x[a] for a in range(3)]
         for a in range(3):
-            moments[s, a * vectors : (a + 1) * vectors, :] = wide[s, a]
+            moments[s, a * vectors : (a + 1) * vectors, :] = held[a]
         for k, part in enumerate(parts):
             high, low = halves(part)
             place = (3 + k) * vectors
@@ -253,8 +251,8 @@
             moments[s, place : place + vectors, :] = low
 
     def prepare_rows(side, leaf):
-        fill(centred(sites, side, leaf, leaves, centre), -2.0, False)
-        source_rows[side * leaves + leaf] = rows[...].T.astype(BF16)
+        fill(centred(positions, side, leaf, centre), -2.0, False)
+        source_rows[side * leaves + leaf, :, :USED] = rows[:USED, :].T.astype(BF16)
 
     def kernel_matrix(site, target):
         radius = jnp.dot(source_rows[site], target, preferred_element_type=F32)
@@ -266,7 +264,7 @@
     def _(t):
         prepare(1, t)
         prepare_rows(1, t)
-        fill(centred(sites, 1, t, leaves, centre), 1.0, True)
+        fill(centred(positions, 1, t, centre), 1.0, True)
         target_rows[t] = rows[...].astype(BF16)
 
     @pl.loop(0, leaves)
@@ -276,11 +274,11 @@
 
     @pl.when(me > 0)
     def _():
-        halo(0, before)[0].wait_recv()
+        halo(0, 0, before).wait_recv()
 
     @pl.when(me < n - 1)
     def _():
-        halo(1, after)[0].wait_recv()
+        halo(1, 0, after).wait_recv()
 
     for copy in list_loads:
         copy.wait()
@@ -337,11 +335,13 @@
 
     @pl.when(me > 0)
     def _():
-        halo(0, before)[1].wait_recv()
+        for part in (1, 2):
+            halo(0, part, before).wait_recv()
 
     @pl.when(me < n - 1)
     def _():
-        halo(1, after)[1].wait_recv()
+        for part in (1, 2):
+            halo(1, part, after).wait_recv()
 
     @pl.loop(0, leaves)
     def _(t):
@@ -357,9 +357,9 @@
             jnp.concatenate(values, axis=1), matrices[t], preferred_element_type=F32
         )
 
-        point = centred(sites, 1, t, leaves, centre)
+        point = centred(positions, 1, t, centre)
         norm = square(point) + 1.0
-        root = jnp.sqrt(polar[pl.ds(t, 1), :])
+        root = jnp.sqrt(polar[1, pl.ds(t, 1), :])
 
         def group(k):
             return total[t, k * vectors : (k + 1) * vectors, :]
@@ -385,13 +385,13 @@
 
     @pl.when(me < n - 1)
     def _():
-        for copy in halo(0, after):
-            copy.wait_send()
+        for part in range(3):
+            halo(0, part, after).wait_send()
 
     @pl.when(me > 0)
     def _():
-        for copy in halo(1, before):
-            copy.wait_send()
+        for part in range(3):
+            halo(1, part, before).wait_send()
 
 
 def shards(
@@ -415,7 +415,6 @@
     basis = jnp.transpose(basis, (0, 2, 1, 3))
     positions = jnp.transpose(positions, (1, 0, 2))
     rank = leaf_transfer.shape[1]
-    site_rows = -(-3 * leaves // 8) * 8
     groups = 27 * vectors
     slots = cluster_coupling.shape[1]
 
@@ -428,16 +427,15 @@
         in_specs=[ANY] * 12,
         out_specs=pl.BlockSpec(memory_space=pltpu.VMEM),
         scratch_shapes=[
-            like(probes),
-            like(positions),
-            like(polar),
+            pltpu.VMEM((3, *probes.shape), BF16),
+            pltpu.VMEM((3, *positions.shape), F32),
+            pltpu.VMEM((3, *polar.shape), F32),
             like(basis),
             like(leaf_transfer),
             like(cluster_transfer),
             like(upper_transfer),
             pltpu.VMEM((UP + 1, slots, rank, rank), BF16),
-            pltpu.VMEM((3 * leaves, 3, vectors, leaf_size), BF16),
-            pltpu.VMEM((3, site_rows, leaf_size), F32),
+            like(probes),
             pltpu.VMEM((n, vectors, 2 * rank), F32),
             pltpu.VMEM((3 * leaves + 1, groups, leaf_size), BF16),
             pltpu.VMEM((3 * leaves, leaf_size, FEATURES), BF16),
@@ -453,8 +451,8 @@
             pltpu.SemaphoreType.DMA((UP + 1,)),
             pltpu.SemaphoreType.DMA((n,)),
             pltpu.SemaphoreType.DMA((n,)),
-            pltpu.SemaphoreType.DMA((2, 2)),
-            pltpu.SemaphoreType.DMA((2, 2)),
+            pltpu.SemaphoreType.DMA((2, 3)),
+            pltpu.SemaphoreType.DMA((2, 3)),
         ],
         compiler_params=pltpu.CompilerParams(
             collective_id=0, has_side_effects=True, vmem_limit_bytes=56 << 20

time: 30.3 us -> 30.6 us (level)
  Pallas kernels: 28.5 us -> 28.9 us
    pallas_call x1, Pallas kernels: 28.5 us -> 28.9 us  [shards(): pl.pallas_call(functools.partial(apply_operator, n, minor), out_shape=jax...]
where the time goes in v4:
time: 30.6 us; the launch traced here: 30.5 us
  Pallas kernels  28.9 us (94%)
  local copies, waits for them, and re-layouts  1.62 us (5%)
    pallas_call x1, Pallas kernels, shards(): pl.pallas_call(functools.partial(apply_operator, n, minor), out_shape=jax...  28.9 us
    unnamed x1, local copies, waits for them, and re-layouts  1.62 us

profile of v4, /device:TPU:0, one launch (start us, length us, event | category | flops | bytes accessed | tf_op | source)
XLA Modules:
  0.0 30.5 jit_solution(7405071101882389180)
XLA Ops:
  0.0 28.9 %apply_operator.1 = bf16[4,3,16,512]{3,2,1,0:T(8,128)(2,1)} custom-call(bf16[4,3,16,512]{3,2,1,0:T(8,128)(2,1)} %bitcast.7, f32[3,4,512]{2,1,0:T(4,128)} %bitcast.8, f32[4,512]{1,0:T(4,128)} %polar_hbm.1, bf16[4,3,64,512]{3,2,1,0:T(8,128)(2,1)} %bitcast.6, bf16[4,64,64]{2,1,0:T(8,128)(2,1)} %leaf_transfer_hbm.1, bf16[1,64,64]{2,1,0:T(8,128)(2,1)} %cluster_transfer_hbm.1, ...), custom_call_target="tpu_custom_call" | custom-call | tf_op jit(solution)/shard_map/apply_operator/pallas_call | solution.py:424
  28.9 1.6 %copy.14 = bf16[4,16,3,512]{3,1,2,0:T(8,128)(2,1)} copy(bf16[4,16,3,512]{3,1,2,0:T(8,128)(2,1)} %bitcast.5) | data formatting | bytes 393216

commit v5 on v4

--- a/solution.py
+++ b/solution.py
@@ -338,15 +338,18 @@
         for part in (1, 2):
             halo(0, part, before).wait_recv()
 
+        @pl.loop(0, leaves)
+        def _(t):
+            prepare(0, t)
+
     @pl.when(me < n - 1)
     def _():
         for part in (1, 2):
             halo(1, part, after).wait_recv()
 
-    @pl.loop(0, leaves)
-    def _(t):
-        prepare(0, t)
-        prepare(2, t)
+        @pl.loop(0, leaves)
+        def _(t):
+            prepare(2, t)
 
     for t in range(leaves):
         values = []

time: 30.6 us -> 30.3 us (level)
  Pallas kernels: 28.9 us -> 28.5 us
    pallas_call x1, Pallas kernels: 28.9 us -> 28.5 us  [shards(): pl.pallas_call(functools.partial(apply_operator, n, minor), out_shape=jax...]
where the time goes in v5:
time: 30.3 us; the launch traced here: 30.2 us
  Pallas kernels  28.5 us (94%)
  local copies, waits for them, and re-layouts  1.62 us (5%)
    pallas_call x1, Pallas kernels, shards(): pl.pallas_call(functools.partial(apply_operator, n, minor), out_shape=jax...  28.5 us
    unnamed x1, local copies, waits for them, and re-layouts  1.62 us

profile of v5, /device:TPU:0, one launch (start us, length us, event | category | flops | bytes accessed | tf_op | source)
XLA Modules:
  0.0 30.2 jit_solution(3285240530286460931)
XLA Ops:
  0.0 28.5 %apply_operator.1 = bf16[4,3,16,512]{3,2,1,0:T(8,128)(2,1)} custom-call(bf16[4,3,16,512]{3,2,1,0:T(8,128)(2,1)} %bitcast.7, f32[3,4,512]{2,1,0:T(4,128)} %bitcast.8, f32[4,512]{1,0:T(4,128)} %polar_hbm.1, bf16[4,3,64,512]{3,2,1,0:T(8,128)(2,1)} %bitcast.6, bf16[4,64,64]{2,1,0:T(8,128)(2,1)} %leaf_transfer_hbm.1, bf16[1,64,64]{2,1,0:T(8,128)(2,1)} %cluster_transfer_hbm.1, ...), custom_call_target="tpu_custom_call" | custom-call | tf_op jit(solution)/shard_map/apply_operator/pallas_call | solution.py:427
  28.5 1.6 %copy.14 = bf16[4,16,3,512]{3,1,2,0:T(8,128)(2,1)} copy(bf16[4,16,3,512]{3,1,2,0:T(8,128)(2,1)} %bitcast.5) | data formatting | bytes 393216
